TPU v7x, 32 devices: a whole 2x2x4 slice. The times are simulated.
32 devices in a mesh: fsdp: 8 (over z, core), ctx: 2 (over x), tp: 2 (over y).
Axes of the slice: x: 2, y: 2, z: 4, core: 2. Of those that a mesh axis runs over, the one named last changes fastest.
Arguments:
- tokens: bfloat16 [32, 1024, 768], P(('fsdp', 'tp'), 'ctx'), may hold values from -6 to 6
- query_key_value_weight: bfloat16 [768, 2304], P('fsdp'), may hold values from -0.21875 to 0.21875
- output_weight: bfloat16 [768, 768], P('fsdp'), may hold values from -3.5 to 3.5
- gate_weight: bfloat16 [768, 3072], P('fsdp', 'tp'), may hold values from -0.21875 to 0.21875
- up_weight: bfloat16 [768, 3072], P('fsdp', 'tp'), may hold values from -0.21875 to 0.21875
- down_weight: bfloat16 [3072, 768], P('tp', 'fsdp'), may hold values from -0.109375 to 0.109375
- gain_one: bfloat16 [768], P('fsdp'), may hold values from 0.25 to 1.75
- shift_one: bfloat16 [768], P('fsdp'), may hold values from -2.5 to 2.5
- gain_two: bfloat16 [768], P('fsdp'), may hold values from 0.25 to 1.75
- shift_two: bfloat16 [768], P('fsdp'), may hold values from -2.5 to 2.5
- lengths: int32 [32], P(('fsdp', 'tp')), may hold values from 256 to 1024, as said below
- positions: int32 [32, 1024], P(('fsdp', 'tp'), 'ctx'), may hold values from 0 to 2046, as said below
- cotangent: bfloat16 [32, 1024, 768], P(('fsdp', 'tp'), 'ctx'), may hold values from -6 to 6
Outputs:
- mixed_out: bfloat16 [32, 1024, 768], P(('fsdp', 'tp'), 'ctx')
- grad_tokens: float32 [32, 1024, 768], P(('fsdp', 'tp'), 'ctx')
- grad_w_qkv: float32 [768, 2304], P('fsdp')
- grad_w_out: float32 [768, 768], P('fsdp')
- grad_w_gate: float32 [768, 3072], P('fsdp', 'tp')
- grad_w_up: float32 [768, 3072], P('fsdp', 'tp')
- grad_w_down: float32 [3072, 768], P('tp', 'fsdp')
- grad_gain_one: float32 [768], P('fsdp')
- grad_shift_one: float32 [768], P('fsdp')
- grad_gain_two: float32 [768], P('fsdp')
- grad_shift_two: float32 [768], P('fsdp')
Inputs may be any that keep to these rules, and one draw needn't show every extreme that they name: `lengths`: each slot's valid tokens are its first ones; in each aligned block of 2 slots (the slots of one device) at least one slot holds 1024, which one drawn from the seed. `positions`: in each slot the first id is 0 and each next one is 1 or 2 larger; in some slot, drawn from the seed, every step is 2.
All inputs are finite; a program needn't handle non-finite values.
Results may differ from a plain program's by a relative error of at most 0.023.
Values may be sent and summed in bfloat16 or wider, within the bound.
No kernel may reach another device: no remote copies, remote signals or barrier semaphores. Data moves between devices by JAX's collectives and lax.ppermute only.
A program may use at most 192 MiB of HBM per device.

v0:
```python
import functools

import jax
import jax.numpy as jnp
from jax import lax
from jax.experimental import pallas as pl
from jax.experimental.pallas import tpu as pltpu
from jax.sharding import PartitionSpec as P

HEADS = 12
HEAD_DIM = 64
PAIR = 2 * HEAD_DIM

norm_eps = 1e-05
rope_base = 1000.0
masked_bias = -1000000000.0

bf16 = jnp.bfloat16
f32 = jnp.float32
NN = (((1,), (0,)), ((), ()))
NT = (((1,), (1,)), ((), ()))
ANY = pl.BlockSpec(memory_space=pl.ANY)


def dot(left, right, dims=NN):
    return lax.dot_general(left, right, dims, preferred_element_type=f32)


def params(limit=60):
    return pltpu.CompilerParams(vmem_limit_bytes=limit * 2**20)


def cost(flops, moved, exps=0):
    return pl.CostEstimate(flops=int(flops), bytes_accessed=int(moved), transcendentals=int(exps))


def fence(*values, waits=()):
    def nothing(*refs):
        pass

    return pl.pallas_call(
        nothing,
        in_specs=[ANY] * (len(values) + len(waits)),
        out_specs=[ANY] * len(values),
        out_shape=[jax.ShapeDtypeStruct(value.shape, value.dtype) for value in values],
        input_output_aliases={place: place for place in range(len(values))},
        compiler_params=params(),
        name="fence",
    )(*values, *waits)


def piece_copies(own, other, spots, full, sems):
    col_blocks, row_blocks, rows, width = own.shape
    copies = []
    for side, source in enumerate((own, other)):
        for row in range(row_blocks):
            for col in range(col_blocks):
                start = pl.multiple_of(spots[side * row_blocks + row], 16)
                left = pl.multiple_of(spots[2 * row_blocks + col], 128)
                copies.append(
                    pltpu.make_async_copy(
                        source.at[col, row],
                        full.at[pl.ds(start, rows), pl.ds(left, width)],
                        sems.at[(side * row_blocks + row) * col_blocks + col],
                    )
                )
    return copies


def piece_count(own):
    return 2 * own.shape[0] * own.shape[1]


def turned(block, cosine, sine):
    lane = lax.broadcasted_iota(jnp.int32, block.shape, 1)
    first = (lane % HEAD_DIM) < HEAD_DIM // 2
    partner = jnp.where(
        first, pltpu.roll(block, PAIR - HEAD_DIM // 2, 1), pltpu.roll(block, HEAD_DIM // 2, 1)
    )
    return block * cosine + partner * sine


def turn_tables(places):
    half_dim = HEAD_DIM // 2
    frequency = rope_base ** (-jnp.arange(half_dim, dtype=f32) * 2.0 / HEAD_DIM)
    angles = places.astype(f32)[:, None] * frequency
    cosine = jnp.cos(angles)
    sine = jnp.sin(angles)
    return jnp.concatenate([cosine] * 4, 1), jnp.concatenate([-sine, sine, -sine, sine], 1)


def project_kernel(
    spots, tokens, cosine, sine, own, other, q_out, k_out, v_out, tokens_t, weight, sems
):
    width = q_out.shape[1]

    @pl.when(pl.program_id(0) == 0)
    def _():
        copies = piece_copies(own, other, spots, weight, sems)
        for copy in copies:
            copy.start()
        for copy in copies:
            copy.wait()

    rows = tokens[...]
    tokens_t[...] = rows.T
    cos_part = cosine[...]
    sin_part = sine[...]
    for part, out in enumerate((q_out, k_out, v_out)):
        raw = dot(rows, weight[:, part * width : (part + 1) * width])
        for pair in range(width // PAIR):
            cols = slice(pair * PAIR, (pair + 1) * PAIR)
            block = raw[:, cols]
            if part < 2:
                block = turned(block, cos_part, sin_part)
            block = block.astype(bf16)
            if part == 0:
                block = block * jnp.asarray(HEAD_DIM**-0.5, bf16)
            out[:, cols] = block


def project(spots, tokens, cosine, sine, own, other, block=256):
    rows, width = tokens.shape
    total = own.shape[0] * own.shape[3]
    row_spec = pl.BlockSpec((block, width), lambda i, *_: (i, 0))
    table = pl.BlockSpec((block, PAIR), lambda i, *_: (i, 0))
    part = total // 3
    out_spec = pl.BlockSpec((block, part), lambda i, *_: (i, 0))
    return pl.pallas_call(
        project_kernel,
        grid_spec=pltpu.PrefetchScalarGridSpec(
            num_scalar_prefetch=1,
            grid=(rows // block,),
            in_specs=[row_spec, table, table, ANY, ANY],
            out_specs=[out_spec] * 3 + [pl.BlockSpec((width, block), lambda i, *_: (0, i))],
            scratch_shapes=[
                pltpu.VMEM((width, total), bf16),
                pltpu.SemaphoreType.DMA((piece_count(own),)),
            ],
        ),
        out_shape=[jax.ShapeDtypeStruct((rows, part), bf16)] * 3
        + [jax.ShapeDtypeStruct((width, rows), bf16)],
        compiler_params=params(),
        cost_estimate=cost(2 * rows * width * total, 4 * rows * total + 2 * width * total),
        name="project",
    )(spots, tokens, cosine, sine, own, other)


def lane_ids(shape):
    return lax.broadcasted_iota(jnp.int32, shape, 1)


def key_bias(length, shape):
    return jnp.where(lax.broadcasted_iota(jnp.int32, shape, 0) < length, 0.0, masked_bias).astype(
        bf16
    )


def attend_kernel(length, q_ref, k_ref, v_ref, out_ref, summit_ref):
    lane_q = lane_ids(q_ref.shape)
    lane_k = lane_ids(k_ref.shape)
    bias = key_bias(length[0], k_ref.shape)
    queries = q_ref[...]
    keys = k_ref[...]
    values = v_ref[...]
    one = jnp.ones((), bf16)
    zero = jnp.zeros((), bf16)
    outs = []
    summits = []
    for head in range(2):
        mine_q = (lane_q < HEAD_DIM) if head == 0 else (lane_q >= HEAD_DIM)
        mine_k = (lane_k < HEAD_DIM) if head == 0 else (lane_k >= HEAD_DIM)
        spare = HEAD_DIM * (1 - head)
        query = jnp.where(mine_q, queries, jnp.where(lane_q == spare, one, zero))
        key = jnp.where(mine_k, keys, bias)
        value = jnp.where(mine_k, values, one)
        scores = dot(query, key, NT)
        top = jnp.max(scores, axis=1, keepdims=True)
        summed = dot(jnp.exp(scores - top).astype(bf16), value)
        totals = pltpu.roll(summed, HEAD_DIM, 1)
        outs.append(summed / totals)
        summits.append(top + jnp.log(summed))
    low = lane_q < HEAD_DIM
    out_ref[...] = jnp.where(low, outs[0], outs[1]).astype(bf16)
    summit_ref[0] = jnp.where(low, summits[1], summits[0])


def attend(length, queries, keys, values):
    rows, width = queries.shape
    seq = keys.shape[0]
    pairs = width // PAIR
    q_spec = pl.BlockSpec((rows, PAIR), lambda h, *_: (0, h))
    k_spec = pl.BlockSpec((seq, PAIR), lambda h, *_: (0, h))
    return pl.pallas_call(
        attend_kernel,
        grid_spec=pltpu.PrefetchScalarGridSpec(
            num_scalar_prefetch=1,
            grid=(pairs,),
            in_specs=[q_spec, k_spec, k_spec],
            out_specs=[q_spec, pl.BlockSpec((1, rows, PAIR), lambda h, *_: (h, 0, 0))],
        ),
        out_shape=[
            jax.ShapeDtypeStruct((rows, width), bf16),
            jax.ShapeDtypeStruct((pairs, rows, PAIR), f32),
        ],
        compiler_params=params(),
        cost_estimate=cost(16 * rows * seq * width, 12 * rows * width),
        name="attend",
    )(length, queries, keys, values)


def three_parts(value):
    high = value.astype(bf16)
    rest = value - high.astype(f32)
    middle = rest.astype(bf16)
    return high, middle, (rest - middle.astype(f32)).astype(bf16)


def pair_back(length, q_ref, k_ref, v_ref, out_ref, summit_ref, grad_ref):
    rows = q_ref.shape[0]
    lane_q = lane_ids(q_ref.shape)
    lane_k = lane_ids(k_ref.shape)
    bias = key_bias(length[0], k_ref.shape)
    queries = q_ref[...]
    keys = k_ref[...]
    values = v_ref[...]
    grads = grad_ref[...]
    summit = three_parts(summit_ref[0])
    product = grads.astype(f32) * out_ref[...].astype(f32)
    one = jnp.ones((), bf16)
    zero = jnp.zeros((), bf16)
    grads_t = grads.T
    queries_t = queries.T
    dq, dk, dv = [], [], []
    for head in range(2):
        mine_q = (lane_q < HEAD_DIM) if head == 0 else (lane_q >= HEAD_DIM)
        mine_k = (lane_k < HEAD_DIM) if head == 0 else (lane_k >= HEAD_DIM)
        spare = HEAD_DIM * (1 - head)
        own = slice(HEAD_DIM * head, HEAD_DIM * (head + 1))
        row_dot = jnp.sum(jnp.where(mine_q, product, 0.0), axis=1, keepdims=True)
        row_dot = three_parts(jnp.broadcast_to(row_dot, (rows, PAIR)))

        def beside(main, mine, lane, parts, last):
            extra = jnp.where(lane == spare + 3, last, zero)
            for place in range(3):
                extra = jnp.where(lane == spare + place, parts[place], extra)
            return jnp.where(mine, main, extra)

        minus = (-one, -one, -one)
        query = beside(queries, mine_q, lane_q, summit, one)
        key = beside(keys, mine_k, lane_k, minus, bias)
        grad = beside(grads, mine_q, lane_q, row_dot, zero)
        value = beside(values, mine_k, lane_k, minus, zero)
        probs = jnp.exp(dot(query, key, NT))
        grad_scores = (probs * dot(grad, value, NT)).astype(bf16)
        dv.append(dot(grads_t[own], probs.astype(bf16)))
        dk.append(dot(queries_t[own], grad_scores))
        dq.append(dot(grad_scores, keys))
    grad_query = jnp.where(lane_q < HEAD_DIM, dq[0], dq[1]) * HEAD_DIM**-0.5
    return grad_query, jnp.concatenate(dk, 0).T, jnp.concatenate(dv, 0).T


def attend_back_kernel(
    waits,
    length,
    first,
    q_ref,
    k_ref,
    v_ref,
    out_ref,
    summit_ref,
    grad_ref,
    cos_ref,
    sin_ref,
    tokens_t,
    *refs,
):
    outer_ref, raw_ref = refs[-2:]
    grad_query, grad_keys, grad_values = pair_back(
        length, q_ref, k_ref, v_ref, out_ref, summit_ref, grad_ref
    )
    cosine = cos_ref[...]
    sine = sin_ref[...]
    raw = jnp.concatenate(
        [
            turned(grad_query, cosine, -sine).astype(bf16),
            turned(grad_keys, cosine, -sine).astype(bf16),
            grad_values.astype(bf16),
        ],
        1,
    )
    outer_ref[...] = dot(tokens_t[...], raw).astype(bf16)
    raw_ref[...] = raw


def attend_back(
    length,
    queries,
    keys,
    values,
    out,
    summit,
    grads,
    cosine,
    sine,
    tokens_t,
    first,
    pairs,
    waits=(),
    base=None,
):
    rows, width = queries.shape
    q_spec = pl.BlockSpec((rows, PAIR), lambda h, length, first: (0, h + first[0]))
    table = pl.BlockSpec((rows, PAIR), lambda h, *_: (0, 0))
    columns = 3 * PAIR
    if base is None:
        extra, shape, aliases = list(waits), (width, columns * pairs), {}
        outer_spec = pl.BlockSpec((width, columns), lambda h, *_: (0, h))
    else:
        extra, shape = [base] + list(waits), base.shape
        aliases = {11: 0}
        outer_spec = pl.BlockSpec(
            (pl.Element(width), pl.Element(columns)),
            lambda h, length, first: (
                0,
                pl.multiple_of(width + PAIR + (first[0] + h) * columns, PAIR),
            ),
        )
    return pl.pallas_call(
        functools.partial(attend_back_kernel, len(waits)),
        grid_spec=pltpu.PrefetchScalarGridSpec(
            num_scalar_prefetch=2,
            grid=(pairs,),
            in_specs=[
                q_spec,
                q_spec,
                q_spec,
                q_spec,
                pl.BlockSpec((1, rows, PAIR), lambda h, length, first: (h + first[0], 0, 0)),
                q_spec,
                table,
                table,
                pl.BlockSpec(tokens_t.shape, lambda h, *_: (0, 0)),
            ]
            + [ANY] * len(extra),
            out_specs=[
                outer_spec,
                pl.BlockSpec((rows, columns), lambda h, *_: (0, h)),
            ],
        ),
        out_shape=[
            jax.ShapeDtypeStruct(shape, bf16),
            jax.ShapeDtypeStruct((rows, columns * pairs), bf16),
        ],
        input_output_aliases=aliases,
        compiler_params=params(),
        cost_estimate=cost(46 * rows * rows * PAIR * pairs, 16 * rows * PAIR * pairs),
        name="attend_back",
    )(
        length,
        jnp.full((1,), first, jnp.int32),
        queries,
        keys,
        values,
        out,
        summit,
        grads,
        cosine,
        sine,
        tokens_t,
        *extra,
    )


def token_kernel(count, slot_half, spots, *refs):
    raws = refs[:count]
    total_ref, own, other = refs[count : count + 3]
    keep, send, weight, sems = refs[-4:]
    width = total_ref.shape[1]
    step = pl.program_id(0)

    @pl.when(step == 0)
    def _():
        copies = piece_copies(own, other, spots, weight, sems)
        for copy in copies:
            copy.start()
        for copy in copies:
            copy.wait()

    order = [part * width + pair * PAIR for pair in range(width // PAIR) for part in range(3)]
    used = jnp.concatenate([weight[:, left : left + PAIR] for left in order], 1)
    total = total_ref[...]
    left = 0
    for raw in raws:
        size = raw.shape[1]
        total = total + dot(raw[...], used[:, left : left + size], NT)
        left += size

    @pl.when(step < pl.num_programs(0) // 2)
    def _():
        send[...] = total.astype(bf16)

    @pl.when(step >= pl.num_programs(0) // 2)
    def _():
        keep[...] = total


def token_gradient(slot_half, spots, raws, total, own, other, waits=(), block=256):
    rows, width = total.shape
    halves = rows // 2 // block

    def source(i, s):
        return (i + (1 - s[0]) * halves) % (2 * halves)

    def rows_of(value):
        return pl.BlockSpec((block, value.shape[1]), lambda i, s, *_: (source(i, s), 0))

    return pl.pallas_call(
        functools.partial(token_kernel, len(raws)),
        grid_spec=pltpu.PrefetchScalarGridSpec(
            num_scalar_prefetch=2,
            grid=(2 * halves,),
            in_specs=[rows_of(raw) for raw in raws]
            + [rows_of(total), ANY, ANY]
            + [ANY] * len(waits),
            out_specs=[
                pl.BlockSpec((block, width), lambda i, *_: (jnp.maximum(i - halves, 0), 0)),
                pl.BlockSpec((block, width), lambda i, *_: (jnp.minimum(i, halves - 1), 0)),
            ],
            scratch_shapes=[
                pltpu.VMEM((width, 3 * width), bf16),
                pltpu.SemaphoreType.DMA((piece_count(own),)),
            ],
        ),
        out_shape=[
            jax.ShapeDtypeStruct((rows // 2, width), f32),
            jax.ShapeDtypeStruct((rows // 2, width), bf16),
        ],
        compiler_params=params(),
        cost_estimate=cost(6 * rows * width * width, 14 * rows * width + 6 * width * width),
        name="token_gradient",
    )(slot_half, spots, *raws, total, own, other, *waits)


def attend_back_plain_kernel(
    length, q_ref, k_ref, v_ref, out_ref, summit_ref, grad_ref, dq_ref, dk_ref, dv_ref
):
    dq_ref[...], dk_ref[...], dv_ref[...] = pair_back(
        length, q_ref, k_ref, v_ref, out_ref, summit_ref, grad_ref
    )


def attend_back_plain(length, queries, keys, values, out, summit, grads):
    rows, width = queries.shape
    seq = keys.shape[0]
    q_spec = pl.BlockSpec((rows, PAIR), lambda h, *_: (0, h))
    k_spec = pl.BlockSpec((seq, PAIR), lambda h, *_: (0, h))
    return pl.pallas_call(
        attend_back_plain_kernel,
        grid_spec=pltpu.PrefetchScalarGridSpec(
            num_scalar_prefetch=1,
            grid=(width // PAIR,),
            in_specs=[
                q_spec,
                k_spec,
                k_spec,
                q_spec,
                pl.BlockSpec((1, rows, PAIR), lambda h, *_: (h, 0, 0)),
                q_spec,
            ],
            out_specs=[q_spec, k_spec, k_spec],
        ),
        out_shape=[jax.ShapeDtypeStruct((count, width), f32) for count in (rows, seq, seq)],
        compiler_params=params(),
        cost_estimate=cost(40 * rows * seq * width, 16 * rows * width),
        name="attend_back_plain",
    )(length, queries, keys, values, out, summit, grads)


def row_mean(value):
    return jnp.mean(value, axis=-1, keepdims=True)


def normalize(value):
    centered = value - row_mean(value)
    inverse = lax.rsqrt(row_mean(centered * centered) + norm_eps)
    return centered * inverse, inverse


def normalize_back(normed, inverse, gain, upstream):
    scaled = upstream * gain
    return inverse * (scaled - row_mean(scaled) - normed * row_mean(scaled * normed))


def weight_copies(plan, group, sources, weight, spots, sems, chunk):
    copies = [[] for _ in range(weight.shape[1] // chunk)]
    count = 0
    for source, first, top, left, row, col, rows, cols in plan["pieces"][group]:
        dynamic = isinstance(row, tuple)
        if dynamic:
            row = pl.multiple_of(spots[row[0]], 16)
            col = pl.multiple_of(spots[col[0]], 128)
        width = cols if dynamic else min(cols, chunk)
        for inside in range(0, cols, width):
            copy = pltpu.make_async_copy(
                sources[source].at[first, pl.ds(top, rows), pl.ds(left + inside, width)],
                weight.at[pl.ds(row, rows), pl.ds(col + inside, width)],
                sems.at[group, count],
            )
            copies[0 if dynamic else (col + inside) // chunk].append(copy)
            count += 1
    return copies


def weight_copy_count(plan):
    counts = []
    for pieces in plan["pieces"]:
        counts.append(
            sum(
                1 if isinstance(row, tuple) else -(-cols // plan["chunk"])
                for _, _, _, _, row, _, _, cols in pieces
            )
        )
    return max(counts)


def feed_kernel(plan, slot_half, spots_in, spots_out, tokens, context, cotangent, norms, *refs):
    sources = refs[: plan["sources"]]
    (
        mixed_keep,
        mixed_send,
        grad_mix_one,
        grad_context,
        out_ref,
        keep,
        send,
        w_out,
        w_gate,
        w_up,
        w_down,
        slopes,
        known,
        lefts,
        context_t,
        attn_rows,
        vectors,
        stage,
        out_stage,
        sems,
        out_sems,
        out_sem,
    ) = refs[plan["sources"] :]
    chunk = plan["chunk"]
    rows, width = tokens.shape
    steps = known.shape[1] // rows
    step = pl.program_id(0)
    feed_total = w_gate.shape[1]
    chunks = feed_total // chunk
    weights = (w_out, w_gate, w_up, w_down)
    loads = [
        weight_copies(plan, group, sources, weight, spots_in, sems, min(chunk, weight.shape[1]))
        for group, weight in enumerate(weights)
    ]

    @pl.when(step == 0)
    def _():
        order = [loads[0][0]]
        for place in range(chunks):
            order += [loads[1][place], loads[2][place], loads[3][place]]
        for group in order:
            for copy in group:
                copy.start()
        vectors[...] = jnp.zeros_like(vectors)

    def arrive(*groups):
        @pl.when(step == 0)
        def _():
            for group in groups:
                for copy in group:
                    copy.wait()

    @pl.when(step < steps)
    def _():
        here = pl.ds(pl.multiple_of(step * rows, rows), rows)
        gain_one = norms[0:1, :]
        shift_one = norms[1:2, :]
        gain_two = norms[2:3, :]
        shift_two = norms[3:4, :]
        arrive(loads[0][0])
        context_rows = context[...]
        context_t[:, here] = context_rows.T
        normed_one, inverse_one = normalize(
            tokens[...].astype(f32) + dot(context_rows, w_out[...])
        )
        out_one = normed_one * gain_one + shift_one
        feed_in = out_one.astype(bf16)
        lefts[1, :, here] = feed_in.T
        total = out_one
        for place in range(chunks):
            cols = slice(place * chunk, (place + 1) * chunk)
            arrive(loads[1][place], loads[2][place], loads[3][place])
            gate = dot(feed_in, w_gate[:, cols])
            up = dot(feed_in, w_up[:, cols])
            sig = jax.nn.sigmoid(gate)
            swish = gate * sig
            hid = (swish * up).astype(bf16)
            known[0, here, cols] = hid
            slopes[0, :, cols] = swish.astype(bf16)
            slopes[1, :, cols] = (up * (sig + swish * (1.0 - sig))).astype(bf16)
            total = total + dot(hid, w_down[:, cols], NT)
        normed_two, inverse_two = normalize(total)
        mixed = (normed_two * gain_two + shift_two).astype(bf16)

        @pl.when(step < steps // 2)
        def _():
            mixed_send[...] = mixed

        @pl.when(step >= steps // 2)
        def _():
            mixed_keep[...] = mixed

        upstream = cotangent[...].astype(f32)
        grad_mix_two = normalize_back(normed_two, inverse_two, gain_two, upstream)
        branch = grad_mix_two.astype(bf16)
        lefts[0, :, here] = branch.T
        grad_out_one = grad_mix_two
        for place in range(chunks):
            cols = slice(place * chunk, (place + 1) * chunk)
            grad_hidden = dot(branch, w_down[:, cols])
            grad_gate = (grad_hidden * slopes[1, :, cols].astype(f32)).astype(bf16)
            grad_up = (grad_hidden * slopes[0, :, cols].astype(f32)).astype(bf16)
            known[1, here, cols] = grad_gate
            known[2, here, cols] = grad_up
            grad_out_one = (
                grad_out_one
                + dot(grad_gate, w_gate[:, cols], NT)
                + dot(grad_up, w_up[:, cols], NT)
            )
        vectors[0:1, :] += jnp.sum(grad_out_one * normed_one, axis=0, keepdims=True)
        vectors[1:2, :] += jnp.sum(grad_out_one, axis=0, keepdims=True)
        vectors[2:3, :] += jnp.sum(upstream * normed_two, axis=0, keepdims=True)
        vectors[3:4, :] += jnp.sum(upstream, axis=0, keepdims=True)
        grad_one = normalize_back(normed_one, inverse_one, gain_one, grad_out_one)
        grad_mix_one[...] = grad_one
        grad_rows = grad_one.astype(bf16)
        attn_rows[here, :] = grad_rows
        grad_context[...] = dot(grad_rows, w_out[...], NT).astype(bf16)

    _, col_blocks, row_blocks, piece_rows, _ = keep.shape
    per = chunks // col_blocks

    def piece_moves(place):
        job, inside = place // chunks, place % chunks
        col, left = inside // per, inside % per * chunk
        slot = place % 2
        moves = []
        for side, out in enumerate((keep, send)):
            for row in range(row_blocks):
                start = pl.multiple_of(spots_out[side * row_blocks + row], 16)
                moves.append(
                    pltpu.make_async_copy(
                        stage.at[slot, pl.ds(start, piece_rows), :],
                        out.at[job, col, row, :, pl.ds(pl.multiple_of(left, 128), chunk)],
                        out_sems.at[slot, side * row_blocks + row],
                    )
                )
        return moves

    @pl.when(step >= steps)
    def _():
        place = step - steps

        @pl.when(place >= 2)
        def _():
            for move in piece_moves(place - 2):
                move.wait()

        job, inside = place // chunks, place % chunks
        start = spots_out[2 * row_blocks + inside // per] + inside % per * chunk
        cols = pl.ds(pl.multiple_of(start, 128), chunk)
        left_t = lefts[jnp.minimum(job, 1)]
        stage[place % 2] = dot(left_t, known[job, :, cols]).astype(bf16)
        for move in piece_moves(place):
            move.start()

    @pl.when(step == pl.num_programs(0) - 1)
    def _():
        out_stage[:, :width] = dot(context_t[...], attn_rows[...]).astype(bf16)
        out_stage[:, width:] = vectors[...].astype(bf16).T
        move = pltpu.make_async_copy(out_stage, out_ref.at[:, pl.ds(0, width + PAIR)], out_sem)
        move.start()
        move.wait()
        for place in (3 * chunks - 2, 3 * chunks - 1):
            for move in piece_moves(place):
                move.wait()


def feed_forward(
    plan,
    sources,
    slot_half,
    spots_in,
    spots_out,
    tokens,
    context,
    cotangent,
    norms,
    feed_total,
    pieces,
    more,
    block=256,
):
    rows, width = tokens.shape
    half = rows // 2
    halves = half // block
    chunk = plan["chunk"]
    chunks = 3 * feed_total // chunk

    def source(i, s):
        return (jnp.minimum(i, 2 * halves - 1) + (1 - s[0]) * halves) % (2 * halves)

    row_spec = pl.BlockSpec((block, width), lambda i, s, *_: (source(i, s), 0))
    keep_spec = pl.BlockSpec((block, width), lambda i, *_: (jnp.clip(i - halves, 0, halves - 1), 0))
    send_spec = pl.BlockSpec((block, width), lambda i, *_: (jnp.minimum(i, halves - 1), 0))
    whole = pl.BlockSpec((8, width), lambda i, *_: (0, 0))
    return pl.pallas_call(
        functools.partial(feed_kernel, plan),
        grid_spec=pltpu.PrefetchScalarGridSpec(
            num_scalar_prefetch=3,
            grid=(rows // block + chunks,),
            in_specs=[row_spec, row_spec, row_spec, whole] + [ANY] * len(sources),
            out_specs=[
                keep_spec,
                send_spec,
                row_spec,
                row_spec,
                ANY,
            ]
            + [ANY] * 2,
            scratch_shapes=[pltpu.VMEM((width, width), bf16)]
            + [pltpu.VMEM((width, feed_total), bf16)] * 3
            + [
                pltpu.VMEM((2, block, feed_total), bf16),
                pltpu.VMEM((3, rows, feed_total), bf16),
                pltpu.VMEM((2, width, rows), bf16),
                pltpu.VMEM((width, rows), bf16),
                pltpu.VMEM((rows, width), bf16),
                pltpu.VMEM((PAIR, width), f32),
                pltpu.VMEM((2, width, chunk), bf16),
                pltpu.VMEM((width, width + PAIR), bf16),
                pltpu.SemaphoreType.DMA((4, weight_copy_count(plan))),
                pltpu.SemaphoreType.DMA((2, 2 * pieces[1])),
                pltpu.SemaphoreType.DMA,
            ],
        ),
        out_shape=[
            jax.ShapeDtypeStruct((half, width), bf16),
            jax.ShapeDtypeStruct((half, width), bf16),
            jax.ShapeDtypeStruct((rows, width), f32),
            jax.ShapeDtypeStruct((rows, width), bf16),
            jax.ShapeDtypeStruct((width, width + PAIR + more), bf16),
        ]
        + [jax.ShapeDtypeStruct((3,) + pieces, bf16)] * 2,
        compiler_params=pltpu.CompilerParams(vmem_limit_bytes=62 * 2**20),
        cost_estimate=cost(
            2 * rows * width * (9 * feed_total + 3 * width),
            rows * 24 * width + 12 * width * feed_total,
        ),
        name="feed_forward",
    )(slot_half, spots_in, spots_out, tokens, context, cotangent, norms, *sources)


class Transfers:
    def __init__(self, mesh):
        self.fsdp = mesh.shape["fsdp"]
        self.ctx = mesh.shape["ctx"]
        self.tp = mesh.shape["tp"]
        self.levels = self.fsdp // 2
        place = lax.axis_index("fsdp")
        self.z = place // 2
        self.core = place % 2
        self.x = lax.axis_index("ctx")
        self.y = lax.axis_index("tp")
        self.paired = self.ctx == 2 and self.tp == 2 and self.fsdp % 2 == 0

    def swap_slots(self, value):
        return lax.ppermute(value, "ctx", [(i, i ^ 1) for i in range(self.ctx)])

    def swap(self, value, axis):
        return lax.ppermute(value, axis, [(0, 1), (1, 0)])

    def swap_core(self, value):
        return lax.ppermute(value, "fsdp", [(i, i ^ 1) for i in range(self.fsdp)])

    def shift(self, value, step):
        pairs = [
            (2 * level + core, 2 * ((level + step) % self.levels) + core)
            for level in range(self.levels)
            for core in range(2)
        ]
        return lax.ppermute(value, "fsdp", pairs)

    def spots(self, rows, sign, width=None):
        found = []
        for side in range(2):
            for part in range(2):
                for step in range(self.levels):
                    level = (self.z + sign * step + self.levels) % self.levels
                    block = 2 * level + jnp.bitwise_xor(self.core, side)
                    found.append(2 * rows * block + rows * jnp.bitwise_xor(self.x, part))
        if width is None:
            found = found + [jnp.zeros((), jnp.int32)]
        else:
            found = found + [self.y * width, (1 - self.y) * width]
        return jnp.stack(found).astype(jnp.int32)

    def mine(self, shard):
        half = shard.shape[0] // 2
        return lax.dynamic_slice_in_dim(shard, self.x * half, half, 0)

    def shifts(self, block):
        return [self.shift(block, step) for step in range(1, self.levels)]

    def gather_feed(self, gate, up, out, norms):
        rows, width = gate.shape
        model = out.shape[1]
        share = rows // self.tp
        block = lax.dynamic_slice_in_dim(out, self.y * share, share, 0)
        tail = jnp.concatenate([block[16 * j : 16 * (j + 1)] for j in range(share // 16)], 1)
        norm_tail = jnp.pad(norms, ((0, 16 - norms.shape[0]), (0, 2 * width - tail.shape[1] - rows)))
        packed = jnp.concatenate(
            [jnp.concatenate([gate, up], 1), jnp.concatenate([tail, norm_tail], 1)], 0
        )
        packed = lax.all_gather(packed, ("fsdp", "tp"), axis=0)
        pieces = [[], [], [], []]
        for place in range(self.fsdp * self.tp):
            row, col = rows * (place // self.tp), width * (place % self.tp)
            for group in range(2):
                pieces[1 + group].append((0, place, 0, group * width, row, col, rows, width))
            for j in range(share // 16):
                row = rows * (place // self.tp) + share * (place % self.tp) + 16 * j
                pieces[0].append((0, place, rows, model * j, row, 0, 16, model))
        blocks = 2 * self.levels
        for side in range(2):
            for col in range(2):
                for row in range(blocks):
                    pieces[3].append(
                        (
                            1 + side,
                            col * blocks + row,
                            0,
                            0,
                            (side * blocks + row,),
                            (2 * blocks + col,),
                            rows // 2,
                            width,
                        )
                    )
        left = model * (share // 16)
        norms = packed[:: self.tp, rows : rows + norms.shape[0], left : left + rows]
        norms = norms.transpose(1, 0, 2).reshape(norms.shape[1], -1)
        return {"sources": 3, "pieces": pieces, "chunk": 768}, packed, norms

    def add(self, left, right):
        return (left.astype(f32) + right.astype(f32)).astype(bf16)

    def level_shifts(self, value):
        return [self.shift(value[step], step) for step in range(1, self.levels)]

    def sum_shifts(self, value, shifts):
        total = value.astype(f32)
        for other in shifts:
            total = total + other.astype(f32)
        return total.astype(bf16)

    def sum_shards(self, value):
        return lax.psum_scatter(value, "fsdp", scatter_dimension=0, tiled=True)

    def sum_all(self, value):
        corners = [(i, i ^ 3) for i in range(4)]
        over_y = self.swap(value, "tp")
        over_x = self.swap(value, "ctx")
        across = lax.ppermute(value, ("ctx", "tp"), corners)
        here = value.astype(f32) + over_y.astype(f32)
        there = over_x.astype(f32) + across.astype(f32)
        return (here + there).astype(bf16)

    def both(self, value, axis, index):
        other = self.swap(value, axis)
        return jnp.where(index == 0, value, other), jnp.where(index == 0, other, value)


def on_device(
    mesh,
    tokens,
    query_key_value_weight,
    output_weight,
    gate_weight,
    up_weight,
    down_weight,
    gain_one,
    shift_one,
    gain_two,
    shift_two,
    lengths,
    positions,
    cotangent,
):
    move = Transfers(mesh)
    shard, model_width = query_key_value_weight.shape[0], tokens.shape[2]
    feed_width = gate_weight.shape[1]
    slot = move.x % 2
    half_rows = tokens.shape[1]

    def sent(value):
        return lax.dynamic_index_in_dim(value, 1 - slot, 0, keepdims=False)

    def to_slot(value, other):
        keep = lax.dynamic_index_in_dim(value, slot, 0, keepdims=False)
        first = jnp.where(slot == 0, keep, other)
        second = jnp.where(slot == 0, other, keep)
        return jnp.concatenate([first, second], 0)

    def from_slot(keep, other):
        return jnp.where(slot == 0, jnp.stack([keep, other]), jnp.stack([other, keep]))

    other_places = move.swap_slots(sent(positions))
    other_tokens = move.swap_slots(sent(tokens))
    length = jnp.where(slot == 0, lengths[0:1], lengths[1:2])
    slot_half = slot[None].astype(jnp.int32)
    norms = jnp.stack([gain_one, shift_one, gain_two, shift_two])
    feed_total = feed_width * move.tp
    down_turned = down_weight.T
    half = shard // 2
    if move.paired:
        levels = move.levels
        blocks = (2, 2 * levels, half)
        narrow = query_key_value_weight.shape[1] // 2
        attn_in = move.spots(half, -1, narrow)
        feed_in = move.spots(half, -1, feed_width)
        plan, packed, norms = move.gather_feed(gate_weight, up_weight, output_weight, norms)
        qkv = lax.dynamic_slice_in_dim(
            move.mine(query_key_value_weight), move.y * narrow, narrow, 1
        )
        down, qkv, send_cotangent, *parts = fence(
            move.mine(down_turned), qkv, sent(cotangent), *move.shifts(qkv)
        )
        qkv = jnp.stack([qkv] + parts)
        qkv_y = move.swap(qkv, "tp")
        down_parts = move.shifts(down)
        slot_tokens = to_slot(tokens, other_tokens)
        cosine, sine = turn_tables(to_slot(positions, other_places))
        qkv, qkv_y, slot_tokens, cosine, sine = fence(qkv, qkv_y, slot_tokens, cosine, sine)
        qkv = jnp.stack([qkv, qkv_y])
        qkv_x = move.swap(qkv, "ctx")
        qkv, qkv_x, send_cotangent, down, *down_parts = fence(
            qkv, qkv_x, send_cotangent, down, *down_parts
        )
        other_cotangent = move.swap_slots(send_cotangent)
        qkv = jnp.stack([qkv, qkv_x], 1).reshape(2, 2 * levels, half, narrow)
        qkv_w = qkv, move.swap_core(qkv)
        down = jnp.stack([down] + down_parts)
        down_y = move.swap(down, "tp")
    else:
        middle = model_width // 2
        attn_in = jnp.asarray([0, middle, 0], jnp.int32)
        feed_in = attn_in

        def whole(value, axes):
            value = lax.all_gather(value, "fsdp", axis=0, tiled=True)
            if axes:
                value = lax.all_gather(value, "tp", axis=1, tiled=True)
            return value[None]

        sources = [
            whole(output_weight, False),
            whole(gate_weight, True),
            whole(up_weight, True),
            whole(down_turned, True),
        ]
        plan = {
            "sources": 4,
            "chunk": 768,
            "pieces": [
                [(place, 0, 0, 0, 0, 0) + source.shape[1:]] for place, source in enumerate(sources)
            ],
        }
        qkv_all = whole(query_key_value_weight, False)
        qkv_w = qkv_all[None, :, :middle], qkv_all[None, :, middle:]
        norms = lax.all_gather(norms, "fsdp", axis=1, tiled=True)
        other_cotangent = move.swap_slots(sent(cotangent))
        slot_tokens = to_slot(tokens, other_tokens)
        cosine, sine = turn_tables(to_slot(positions, other_places))
    norms = jnp.pad(norms.astype(f32), ((0, 4), (0, 0)))

    queries, key_rows, values, tokens_t = project(attn_in, slot_tokens, cosine, sine, *qkv_w)
    if move.paired:
        queries, down, down_y = fence(queries, down, down_y)
        down = jnp.stack([down, down_y])
        down_x = move.swap(down, "ctx")
    mates = move.ctx // 2
    if mates > 1:
        groups = [[2 * j + s for j in range(mates)] for s in range(2)]

        def gather_rows(value):
            return lax.all_gather(value, "ctx", axis=0, tiled=True, axis_index_groups=groups)

        key_rows = gather_rows(key_rows)
        values = gather_rows(values)
    context, summit = attend(length, queries, key_rows, values)
    if move.paired:
        context, down, down_x, other_cotangent = fence(context, down, down_x, other_cotangent)
        down = jnp.stack([down, down_x], 1).reshape(4 * levels, half, feed_width)
        down = down.reshape((2 * 2 * levels, half, feed_width))
        sources = [packed, down, move.swap_core(down)]
    slot_cotangent = to_slot(cotangent, other_cotangent)
    pieces = (2, 2 * levels, half, feed_width) if move.paired else (1, 1, middle, feed_total)
    feed_out = move.spots(half, 1, feed_width) if move.paired else attn_in
    (
        mixed_keep,
        mixed_send,
        grad_mix_one,
        grad_context,
        attn_o,
        feed_keep,
        feed_send,
    ) = feed_forward(
        plan,
        sources,
        slot_half,
        feed_in,
        feed_out,
        slot_tokens,
        context,
        slot_cotangent,
        norms,
        feed_total,
        pieces,
        4 * 3 * PAIR if move.paired else 0,
    )

    pairs = model_width // PAIR
    if move.paired:
        def back(first, count, grads, waits=(), base=None):
            return attend_back(
                length,
                queries,
                key_rows,
                values,
                context,
                summit,
                grads,
                cosine,
                sine,
                tokens_t,
                first,
                count,
                waits,
                base,
            )

        feed_core = move.swap_core(feed_send)
        other_mixed = move.swap_slots(mixed_send)
        attn_a, raw_0 = back(0, 2, grad_context, (), attn_o)

        raw_0, feed_keep, grad_context = fence(
            raw_0, feed_keep, grad_context, waits=(feed_core, other_mixed)
        )
        width = feed_width // 2
        shape = (3, 2, 2, levels, half, feed_width)
        feed_keep, feed_core = feed_keep.reshape(shape), feed_core.reshape(shape)

        def joined(job, place):
            return move.add(feed_keep[job][place], feed_core[job][place])

        every = slice(None)
        first, last = (..., slice(0, width)), (..., slice(width, None))
        down_send = joined(0, (every, 1))
        down_x = move.swap(down_send, "ctx")
        gate_send = joined(1, (1,))
        gate_y = move.swap(gate_send, "tp")
        up_a_send = joined(2, (every, 1) + first)
        up_a_x = move.swap(up_a_send, "ctx")
        up_b_send = joined(2, (1,) + last)
        up_b_y = move.swap(up_b_send, "tp")
        down, gate = joined(0, (every, 0)), joined(1, (0,))
        up_a, up_b = joined(2, (every, 0) + first), joined(2, (0,) + last)
        sends = (down_send, gate_send, up_a_send, up_b_send)
        attn_a, raw_1 = back(2, 2, grad_context, (raw_0, *sends), attn_a)

        raw_1, attn_a, grad_context, down, gate = fence(
            raw_1, attn_a, grad_context, down, gate, waits=(down_x, gate_y)
        )
        attn_a = move.sum_shards(attn_a)
        down_send, down = move.add(down[1], down_x[1]), move.add(down[0], down_x[0])
        gate_send, gate = move.add(gate[1], gate_y[1]), move.add(gate[0], gate_y[0])
        down_y = move.swap(down_send, "tp")
        gate_x = move.swap(gate_send, "ctx")
        attn_c, raw_2 = back(4, 2, grad_context, (down_send, gate_send))

        raw_2, attn_c, down, gate, up_a, up_b = fence(
            raw_2, attn_c, down, gate, up_a, up_b, waits=(down_y, gate_x, up_a_x, up_b_y)
        )
        attn_c = move.sum_shards(attn_c)
        up_a_send, up_a = move.add(up_a[1], up_a_x[1]), move.add(up_a[0], up_a_x[0])
        up_b_send, up_b = move.add(up_b[1], up_b_y[1]), move.add(up_b[0], up_b_y[0])
        up_a_y = move.swap(up_a_send, "tp")
        up_b_x = move.swap(up_b_send, "ctx")
        some = jnp.concatenate([move.add(down, down_y), move.add(gate, gate_x)], 2)
        some_shifts = move.level_shifts(some)
        keep_rows, send_rows = token_gradient(
            slot_half,
            attn_in,
            (raw_0, raw_1, raw_2),
            grad_mix_one,
            *qkv_w,
            (up_a_send, up_b_send, some),
        )

        send_rows, up_a, up_b, attn_a, some = fence(
            send_rows, up_a, up_b, attn_a, some[0], waits=(up_a_y, up_b_x)
        )
        attn_x = move.swap(attn_a, "ctx")
        other_rows = move.swap_slots(send_rows)
        up = jnp.concatenate([move.add(up_a, up_a_y), move.add(up_b, up_b_x)], 2)

        up, attn_a, some = fence(up, attn_a, some, waits=(attn_x, *some_shifts))
        up_shifts = move.level_shifts(up)
        some = move.sum_shifts(some, some_shifts)
        attn_a = move.add(attn_a, attn_x)
        attn_y = move.swap(attn_a, "tp")

        up, attn_a, attn_c, some = fence(
            up[0], attn_a, attn_c, some, waits=(attn_y, *up_shifts)
        )
        feed = jnp.concatenate([some, move.sum_shifts(up, up_shifts)], 1)
        feed_x = move.swap(feed, "ctx")
        attn_a = move.add(attn_a, attn_y)
        attn_c = move.sum_all(attn_c)
        low = jnp.where(move.x == 0, feed, feed_x)
        high = jnp.where(move.x == 0, feed_x, feed)
        feed = jnp.concatenate([low, high], 0).astype(f32)
        attn = attn_a
        down_gradient = feed[:, :feed_width].T
        gate_gradient = feed[:, feed_width : 2 * feed_width]
        up_gradient = feed[:, 2 * feed_width :]
        out_gradient = attn[:, :model_width].astype(f32)
        vector_grads = [attn[:, model_width + place].astype(f32) for place in range(4)]
        attn = jnp.concatenate([attn[:, model_width + PAIR :], attn_c], 1)
        qkv_gradient = attn.reshape(shard, pairs, 3, PAIR).transpose(0, 2, 1, 3)
        qkv_gradient = qkv_gradient.reshape(shard, 3 * model_width).astype(f32)
        mixed_out = from_slot(mixed_keep, other_mixed)
        grad_tokens = from_slot(keep_rows, other_rows.astype(f32))
    else:
        mixed_out = from_slot(mixed_keep, move.swap_slots(mixed_send))
        grad_query, grad_keys, grad_values = attend_back_plain(
            length, queries, key_rows, values, context, summit, grad_context
        )
        if mates > 1:

            def scatter_rows(value):
                return lax.psum_scatter(
                    value, "ctx", scatter_dimension=0, axis_index_groups=groups, tiled=True
                )

            grad_keys, grad_values = scatter_rows(grad_keys), scatter_rows(grad_values)

        def turn_back(value):
            value = value.reshape(-1, HEADS, 2, HEAD_DIM // 2)
            ahead, behind = value[:, :, 0], value[:, :, 1]
            cos_half = cosine[:, None, : HEAD_DIM // 2]
            sin_half = sine[:, None, HEAD_DIM // 2 : HEAD_DIM]
            value = jnp.stack(
                [ahead * cos_half + behind * sin_half, behind * cos_half - ahead * sin_half], 2
            )
            return value.reshape(-1, model_width)

        grad_raw = jnp.concatenate(
            [turn_back(grad_query), turn_back(grad_keys), grad_values], 1
        ).astype(bf16)
        total = grad_mix_one + dot(grad_raw, qkv_all[0], NT)
        first = lax.dynamic_slice_in_dim(total, slot * half_rows, half_rows, 0)
        second = lax.dynamic_slice_in_dim(total, (1 - slot) * half_rows, half_rows, 0)
        other_rows = move.swap_slots(second.astype(bf16))
        grad_tokens = from_slot(first, other_rows.astype(f32))
        every = ("ctx", "tp")

        def scatter(value, split):
            value = lax.psum(value, every)
            value = lax.psum_scatter(value, "fsdp", scatter_dimension=0, tiled=True)
            if split:
                value = lax.dynamic_slice_in_dim(value, move.y * feed_width, feed_width, 1)
            return value.astype(f32)

        feed = jnp.concatenate([feed_keep[:, 0, 0], feed_send[:, 0, 0]], 1)
        down_gradient = scatter(feed[0], True).T
        gate_gradient = scatter(feed[1], True)
        up_gradient = scatter(feed[2], True)
        outer = dot(slot_tokens, grad_raw, (((0,), (0,)), ((), ())))
        qkv_gradient = scatter(outer.astype(bf16), False)
        attn_o = scatter(attn_o, False)
        out_gradient = attn_o[:, :model_width]
        vector_grads = [attn_o[:, model_width + place] for place in range(4)]
    return (
        mixed_out,
        grad_tokens,
        qkv_gradient,
        out_gradient,
        gate_gradient,
        up_gradient,
        down_gradient,
        *vector_grads,
    )


def solution(mesh):
    in_specs = (
        P(("fsdp", "tp"), "ctx", None),
        P("fsdp", None),
        P("fsdp", None),
        P("fsdp", "tp"),
        P("fsdp", "tp"),
        P("tp", "fsdp"),
        P("fsdp"),
        P("fsdp"),
        P("fsdp"),
        P("fsdp"),
        P(("fsdp", "tp")),
        P(("fsdp", "tp"), "ctx"),
        P(("fsdp", "tp"), "ctx", None),
    )
    out_specs = (
        P(("fsdp", "tp"), "ctx", None),
        P(("fsdp", "tp"), "ctx", None),
        P("fsdp", None),
        P("fsdp", None),
        P("fsdp", "tp"),
        P("fsdp", "tp"),
        P("tp", "fsdp"),
        P("fsdp"),
        P("fsdp"),
        P("fsdp"),
        P("fsdp"),
    )
    return jax.shard_map(
        functools.partial(on_device, mesh),
        mesh=mesh,
        in_specs=in_specs,
        out_specs=out_specs,
        check_vma=False,
    )
```

profile of v0, /device:TPU:0, one launch (start us, length us, event | category | flops | bytes accessed | tf_op | source)
XLA Modules:
  0.0 394.1 jit_solution(15970459572336114569)
XLA Ops:
  11.3 5.1 %collective-permute-start.2 = (bf16[48,1152]{1,0:T(8,128)(2,1)S(1)}, bf16[48,1152]{1,0:T(8,128)(2,1)S(1)}, u32[]{:S(2)}, u32[]{:S(2)}) collective-permute-start(bf16[48,1152]{1,0:T(8,128)(2,1)S(1)} %dynamic_slice.31.refs_1_), channel_id=1, source_target_pairs={{0,24},{4,28},{8,0},{12,4},{16,8},{20,12},{24,16},{28,20},{1,25},{... | collective-permute-start | bytes 331784 | tf_op jit(solution)/shard_map/ppermute | solution.py:801
  25.3 4.0 %collective-permute-done.1.refs_4_ = bf16[48,1152]{1,0:T(8,128)(2,1)S(1)} collective-permute-done((bf16[48,1152]{1,0:T(8,128)(2,1)S(1)}, bf16[48,1152]{1,0:T(8,128)(2,1)S(1)}, u32[]{:S(2)}, u32[]{:S(2)}) %collective-permute-start.1) | collective-permute-done | bytes 110624 | tf_op jit(solution)/shard_map/ppermute | solution.py:801
  35.4 2.9 collective-permute-done.4
  44.4 3.3 collective-permute-start.9
  47.7 3.6 collective-permute-start.8
  53.8 7.0 %collective-permute-done.8.refs_5_ = bf16[48,1536]{1,0:T(8,128)(2,1)S(1)} collective-permute-done((bf16[48,1536]{1,0:T(8,128)(2,1)S(1)}, bf16[48,1536]{1,0:T(8,128)(2,1)S(1)}, u32[]{:S(2)}, u32[]{:S(2)}) %collective-permute-start.8) | collective-permute-done | bytes 147488 | tf_op jit(solution)/shard_map/ppermute | solution.py:801
  71.0 10.1 %project.1 = (bf16[1024,768]{1,0:T(8,128)(2,1)}, bf16[1024,768]{1,0:T(8,128)(2,1)}, bf16[1024,768]{1,0:T(8,128)(2,1)}, bf16[768,1024]{1,0:T(8,128)(2,1)}) custom-call(s32[18]{0:T(128)} %stack.278.spots, bf16[1024,768]{1,0:T(8,128)(2,1)} %get-tuple-element.87.tokens, f32[1024,128]{1,0:T(8,128)} %get-tuple-element.88.cosine.cos_ref, ...), custom_call_target="tpu_custom_call" | custom-call | flops 3623878656 | bytes 12976128 | tf_op jit(solution)/shard_map/project/pallas_call | solution.py:129
  81.1 13.4 %collective-permute-done.11.refs_2_ = bf16[4,48,1536]{2,1,0:T(8,128)(2,1)S(1)} collective-permute-done((bf16[4,48,1536]{2,1,0:T(8,128)(2,1)S(1)}, bf16[4,48,1536]{2,1,0:T(8,128)(2,1)S(1)}, u32[]{:S(2)}, u32[]{:S(2)}) %collective-permute-start.11) | collective-permute-done | bytes 589856 | tf_op jit(solution)/shard_map/ppermute | solution.py:790
  97.7 23.5 %attend.1 = (bf16[1024,768]{1,0:T(8,128)(2,1)}, f32[6,1024,128]{2,1,0:T(8,128)}) custom-call(s32[1]{0:T(128)S(6)} %select_n.241.length, bf16[1024,768]{1,0:T(8,128)(2,1)} %get-tuple-element.101.q_ref, bf16[1024,768]{1,0:T(8,128)(2,1)} %get-tuple-element.102.k_ref, bf16[1024,768]{1,0:T(8,128)(2,1)} %get-tuple-element.103.v_ref), custom_call_target="tpu_custom_call" | custom-call | flops 12884901888 | bytes 9437184 | tf_op jit(solution)/shard_map/attend/pallas_call | solution.py:194
  121.2 3.1 collective-permute-done.12.refs_2_
  132.7 76.5 %feed_forward.1 = (bf16[512,768]{1,0:T(8,128)(2,1)}, bf16[512,768]{1,0:T(8,128)(2,1)}, f32[1024,768]{1,0:T(8,128)}, bf16[1024,768]{1,0:T(8,128)(2,1)}, bf16[768,...) custom-call(s32[1]{0:T(128)} %bitcast.slot_half, s32[18]{0:T(128)} %stack.257.spots_in, ...), custom_call_target="tpu_custom_call" | custom-call | flops 47110422528 | bytes 47185920 | tf_op jit(solution)/shard_map/feed_forward/pallas_call | solution.py:726
  210.5 18.7 %attend_back.3 = (bf16[768,2432]{1,0:T(8,128)(2,1)}, bf16[1024,768]{1,0:T(8,128)(2,1)}) custom-call(s32[1]{0:T(128)S(6)} %select_n.241.length, s32[1]{0:T(128)} %constant.222.clone.1.first, bf16[1024,768]{1,0:T(8,128)(2,1)} %get-tuple-element.101.q_ref, bf16[1024,768]{1,0:T(8,128)(2,1)} %get-tuple-element.102.k_ref, ...), custom_call_target="tpu_custom_call", output_to_operand_aliasing={{0}: (11, {})} | custom-call | flops 12348030976 | bytes 4194304 | tf_op jit(solution)/shard_map/attend_back/pallas_call | solution.py:329
  230.4 2.7 fusion.35
  233.1 4.1 %add_convert_fusion = (bf16[1,1,8,48,1536]{4,3,2,1,0:T(8,128)(2,1)}, bf16[1,1,8,48,1536]{4,3,2,1,0:T(8,128)(2,1)S(1)}) fusion(bf16[3,2,8,48,1536]{4,3,2,1,0:T(8,128)(2,1)} %collective-permute-done.16.refs_3_, bf16[3,2,8,48,1536]{4,3,2,1,0:T(8,128)(2,1)} %get-tuple-element.124), kind=kLoop, calls=%fused_computation.2 | loop fusion | flops 4718592 | bytes 7077888 | tf_op jit(solution)/shard_map/convert_element_type | solution.py:865
  238.5 2.7 fusion.36
  247.3 19.1 %attend_back.4 = (bf16[768,2432]{1,0:T(8,128)(2,1)}, bf16[1024,768]{1,0:T(8,128)(2,1)}) custom-call(s32[1]{0:T(128)S(6)} %select_n.241.length, s32[1]{0:T(128)} %constant.223.clone.1.first, bf16[1024,768]{1,0:T(8,128)(2,1)} %get-tuple-element.101.q_ref, bf16[1024,768]{1,0:T(8,128)(2,1)} %get-tuple-element.102.k_ref, ...), custom_call_target="tpu_custom_call", output_to_operand_aliasing={{0}: (11, {})} | custom-call | flops 12348030976 | bytes 4194304 | tf_op jit(solution)/shard_map/attend_back/pallas_call | solution.py:329
  266.4 4.7 %collective-permute-done.17.refs_5_ = bf16[2,4,48,1536]{3,2,1,0:T(8,128)(2,1)S(1)} collective-permute-done((bf16[2,4,48,1536]{3,2,1,0:T(8,128)(2,1)}, bf16[2,4,48,1536]{3,2,1,0:T(8,128)(2,1)S(1)}, u32[]{:S(2)}, u32[]{:S(2)}) %collective-permute-start.17) | collective-permute-done | bytes 1179680 | tf_op jit(solution)/shard_map/ppermute | solution.py:790
  281.4 18.8 %attend_back.5 = (bf16[768,768]{1,0:T(8,128)(2,1)}, bf16[1024,768]{1,0:T(8,128)(2,1)}) custom-call(s32[1]{0:T(128)S(6)} %select_n.241.length, s32[1]{0:T(128)} %constant.224.clone.1.first, bf16[1024,768]{1,0:T(8,128)(2,1)} %get-tuple-element.101.q_ref, bf16[1024,768]{1,0:T(8,128)(2,1)} %get-tuple-element.102.k_ref, ...), custom_call_target="tpu_custom_call" | custom-call | flops 12348030976 | bytes 4194304 | tf_op jit(solution)/shard_map/attend_back/pallas_call | solution.py:329
  309.1 4.2 %collective-permute-start.29 = (bf16[48,3072]{1,0:T(8,128)(2,1)S(1)}, bf16[48,3072]{1,0:T(8,128)(2,1)S(1)}, u32[]{:S(2)}, u32[]{:S(2)}) collective-permute-start(bf16[48,3072]{1,0:T(8,128)(2,1)S(1)} %get-tuple-element.182), channel_id=1, source_target_pairs={{0,24},{4,28},{8,0},{12,4},{16,8},{20,12},{24,16},{28,20},{1,25},{... | collective-permute-start | bytes 884744 | tf_op jit(solution)/shard_map/ppermute | solution.py:801
  316.7 10.9 %token_gradient.1 = (f32[512,768]{1,0:T(8,128)}, bf16[512,768]{1,0:T(8,128)(2,1)}) custom-call(s32[1]{0:T(128)} %bitcast.slot_half, s32[18]{0:T(128)} %stack.278.spots, bf16[1024,768]{1,0:T(8,128)(2,1)} %get-tuple-element.121.refs_1_.refs_0_, bf16[1024,768]{1,0:T(8,128)(2,1)} %get-tuple-element.127.refs_1_, bf16[1024,768]{1,0:T(8,128)(2,1)} %get-tuple-element.133.refs_2_, ...), custom_call_target="tpu_custom_call" | custom-call | flops 3623878656 | bytes 14548992 | tf_op jit(solution)/shard_map/token_gradient/pallas_call | solution.py:418
  333.5 13.7 %collective-permute-done.28.refs_5_ = bf16[48,3072]{1,0:T(8,128)(2,1)S(1)} collective-permute-done((bf16[48,3072]{1,0:T(8,128)(2,1)S(1)}, bf16[48,3072]{1,0:T(8,128)(2,1)S(1)}, u32[]{:S(2)}, u32[]{:S(2)}) %collective-permute-start.28) | collective-permute-done | bytes 294944 | tf_op jit(solution)/shard_map/ppermute | solution.py:801
  358.3 6.0 %reduce-scatter.5.cloned.1.call-done.refs_2_ = bf16[96,768]{1,0:T(8,128)(2,1)} async-done(((bf16[768,768]{1,0:T(8,128)(2,1)}), bf16[96,768]{1,0:T(8,128)(2,1)}) %reduce-scatter.5.cloned.1.call-update) | async-done | bytes 147472 | tf_op jit(solution)/shard_map/reduce_scatter | solution.py:877
  364.3 2.7 collective-permute-done.32.refs_6_
  379.3 6.4 %collective-permute-done.37 = bf16[48,4608]{1,0:T(8,128)(2,1)S(1)} collective-permute-done((bf16[48,4608]{1,0:T(8,128)(2,1)S(1)}, bf16[48,4608]{1,0:T(8,128)(2,1)S(1)}, u32[]{:S(2)}, u32[]{:S(2)}) %collective-permute-start.37) | collective-permute-done | bytes 442400 | tf_op jit(solution)/shard_map/ppermute | solution.py:790
  (298 shorter events, 110.6 us)
Async XLA Ops:
  7.2 124.1 %all-gather.3.cloned.1.call-start = ((), (), s32[]{:S(2)}) async-start(), calls=%async_computation.4 | async-start | bytes 11698176 | tf_op jit(solution)/shard_map/all_gather | solution.py:834
  10.2 317.4 %reduce-scatter.3.cloned.1.call-start = ((), (), s32[]{:S(2)}) async-start(), calls=%async_computation.2 | async-start | bytes 4202496 | tf_op jit(solution)/shard_map/reduce_scatter | solution.py:877
  19.9 18.4 %collective-permute-start.4 = (bf16[512,768]{1,0:T(8,128)(2,1)}, bf16[512,768]{1,0:T(8,128)(2,1)S(1)}, u32[]{:S(2)}, u32[]{:S(2)}) collective-permute-start(bf16[512,768]{1,0:T(8,128)(2,1)} %dynamic-slice_bitcast_fusion), channel_id=1, source_target_pairs={{0,2},{2,0},{1,3},{3,1},{4,6},{6,4},{5,7},{7,5},{8,10},{10,8},{9,1... | collective-permute-start | bytes 2359304 | tf_op jit(solution)/shard_map/ppermute | solution.py:787
  42.8 18.4 %collective-permute-start.6 = (bf16[2,4,48,1152]{3,2,1,0:T(8,128)(2,1)S(1)}, bf16[2,4,48,1152]{3,2,1,0:T(8,128)(2,1)S(1)}, u32[]{:S(2)}, u32[]{:S(2)}) collective-permute-start(bf16[2,4,48,1152]{3,2,1,0:T(8,128)(2,1)S(1)} %pad_maximum_fusion.6.refs_0_), channel_id=1, source_target_pairs={{0,2},{2,0},{1,3},{3,1},{4,6},{6,4},{5,7},{7,5},{8,10},{10,8},{9,1... | collective-permute-start | bytes 2654216 | tf_op jit(solution)/shard_map/ppermute | solution.py:790
  65.7 28.7 %collective-permute-start.11 = (bf16[4,48,1536]{2,1,0:T(8,128)(2,1)S(1)}, bf16[4,48,1536]{2,1,0:T(8,128)(2,1)S(1)}, u32[]{:S(2)}, u32[]{:S(2)}) collective-permute-start(bf16[4,48,1536]{2,1,0:T(8,128)(2,1)S(1)} %pad_maximum_fusion.7.refs_1_), channel_id=1, source_target_pairs={{0,1},{1,0},{2,3},{3,2},{4,5},{5,4},{6,7},{7,6},{8,9},{9,8},{10,11... | collective-permute-start | bytes 1769480 | tf_op jit(solution)/shard_map/ppermute | solution.py:790
  69.7 51.5 %collective-permute-start.13 = (bf16[512,768]{1,0:T(8,128)(2,1)S(1)}, bf16[512,768]{1,0:T(8,128)(2,1)S(1)}, u32[]{:S(2)}, u32[]{:S(2)}) collective-permute-start(bf16[512,768]{1,0:T(8,128)(2,1)S(1)} %copy-done.6), channel_id=1, source_target_pairs={{0,2},{2,0},{1,3},{3,1},{4,6},{6,4},{5,7},{7,5},{8,10},{10,8},{9,1... | collective-permute-start | bytes 2359304 | tf_op jit(solution)/shard_map/ppermute | solution.py:787
  96.6 27.7 %collective-permute-start.12 = (bf16[2,4,48,1536]{3,2,1,0:T(8,128)(2,1)S(1)}, bf16[2,4,48,1536]{3,2,1,0:T(8,128)(2,1)S(1)}, u32[]{:S(2)}, u32[]{:S(2)}) collective-permute-start(bf16[2,4,48,1536]{3,2,1,0:T(8,128)(2,1)S(1)} %pad_maximum_fusion.5.refs_1_), channel_id=1, source_target_pairs={{0,2},{2,0},{1,3},{3,1},{4,6},{6,4},{5,7},{7,5},{8,10},{10,8},{9,1... | collective-permute-start | bytes 3538952 | tf_op jit(solution)/shard_map/ppermute | solution.py:790
  209.3 20.2 %collective-permute-start.16 = (bf16[3,2,8,48,1536]{4,3,2,1,0:T(8,128)(2,1)}, bf16[3,2,8,48,1536]{4,3,2,1,0:T(8,128)(2,1)}, u32[]{:S(2)}, u32[]{:S(2)}) collective-permute-start(bf16[3,2,8,48,1536]{4,3,2,1,0:T(8,128)(2,1)} %get-tuple-element.120), channel_id=1, source_target_pairs={{0,4},{4,0},{8,12},{12,8},{16,20},{20,16},{24,28},{28,24},{1,5},{5... | collective-permute-start | bytes 21233672 | tf_op jit(solution)/shard_map/ppermute | solution.py:793
  209.7 19.8 %collective-permute-start.15 = (bf16[512,768]{1,0:T(8,128)(2,1)}, bf16[512,768]{1,0:T(8,128)(2,1)S(1)}, u32[]{:S(2)}, u32[]{:S(2)}) collective-permute-start(bf16[512,768]{1,0:T(8,128)(2,1)} %get-tuple-element.113), channel_id=1, source_target_pairs={{0,2},{2,0},{1,3},{3,1},{4,6},{6,4},{5,7},{7,5},{8,10},{10,8},{9,1... | collective-permute-start | bytes 2359304 | tf_op jit(solution)/shard_map/ppermute | solution.py:787
  237.2 29.1 %collective-permute-start.18 = (bf16[2,4,48,1536]{3,2,1,0:T(8,128)(2,1)S(1)}, bf16[2,4,48,1536]{3,2,1,0:T(8,128)(2,1)S(1)}, u32[]{:S(2)}, u32[]{:S(2)}) collective-permute-start(bf16[2,4,48,1536]{3,2,1,0:T(8,128)(2,1)S(1)} %bitcast.169), channel_id=1, source_target_pairs={{0,1},{1,0},{2,3},{3,2},{4,5},{5,4},{6,7},{7,6},{8,9},{9,8},{10,11... | collective-permute-start | bytes 3538952 | tf_op jit(solution)/shard_map/ppermute | solution.py:790
  243.4 27.6 %collective-permute-start.17 = (bf16[2,4,48,1536]{3,2,1,0:T(8,128)(2,1)}, bf16[2,4,48,1536]{3,2,1,0:T(8,128)(2,1)S(1)}, u32[]{:S(2)}, u32[]{:S(2)}) collective-permute-start(bf16[2,4,48,1536]{3,2,1,0:T(8,128)(2,1)} %get-tuple-element.170.refs_2_), channel_id=1, source_target_pairs={{0,2},{2,0},{1,3},{3,1},{4,6},{6,4},{5,7},{7,5},{8,10},{10,8},{9,1... | collective-permute-start | bytes 3538952 | tf_op jit(solution)/shard_map/ppermute | solution.py:790
  272.2 92.2 %reduce-scatter.5.cloned.1.call-start = ((), (), s32[]{:S(2)}) async-start(), calls=%async_computation.3 | async-start | bytes 1327104 | tf_op jit(solution)/shard_map/reduce_scatter | solution.py:877
  274.9 25.3 %collective-permute-start.22 = (bf16[2,4,48,768]{3,2,1,0:T(8,128)(2,1)S(1)}, bf16[2,4,48,768]{3,2,1,0:T(8,128)(2,1)S(1)}, u32[]{:S(2)}, u32[]{:S(2)}) collective-permute-start(bf16[2,4,48,768]{3,2,1,0:T(8,128)(2,1)S(1)} %copy-done.62), channel_id=1, source_target_pairs={{0,1},{1,0},{2,3},{3,2},{4,5},{5,4},{6,7},{7,6},{8,9},{9,8},{10,11... | collective-permute-start | bytes 1769480 | tf_op jit(solution)/shard_map/ppermute | solution.py:790
  275.6 24.6 %collective-permute-start.21 = (bf16[2,4,48,768]{3,2,1,0:T(8,128)(2,1)S(1)}, bf16[2,4,48,768]{3,2,1,0:T(8,128)(2,1)S(1)}, u32[]{:S(2)}, u32[]{:S(2)}) collective-permute-start(bf16[2,4,48,768]{3,2,1,0:T(8,128)(2,1)S(1)} %copy-done.61), channel_id=1, source_target_pairs={{0,2},{2,0},{1,3},{3,1},{4,6},{6,4},{5,7},{7,5},{8,10},{10,8},{9,1... | collective-permute-start | bytes 1769480 | tf_op jit(solution)/shard_map/ppermute | solution.py:790
  277.7 24.2 %collective-permute-start.20 = (bf16[4,48,1536]{2,1,0:T(8,128)(2,1)S(1)}, bf16[4,48,1536]{2,1,0:T(8,128)(2,1)S(1)}, u32[]{:S(2)}, u32[]{:S(2)}) collective-permute-start(bf16[4,48,1536]{2,1,0:T(8,128)(2,1)S(1)} %get-tuple-element.172.refs_1_), channel_id=1, source_target_pairs={{0,2},{2,0},{1,3},{3,1},{4,6},{6,4},{5,7},{7,5},{8,10},{10,8},{9,1... | collective-permute-start | bytes 1769480 | tf_op jit(solution)/shard_map/ppermute | solution.py:790
  280.1 21.7 %collective-permute-start.19 = (bf16[4,48,1536]{2,1,0:T(8,128)(2,1)}, bf16[4,48,1536]{2,1,0:T(8,128)(2,1)S(1)}, u32[]{:S(2)}, u32[]{:S(2)}) collective-permute-start(bf16[4,48,1536]{2,1,0:T(8,128)(2,1)} %get-tuple-element.174.refs_0_), channel_id=1, source_target_pairs={{0,1},{1,0},{2,3},{3,2},{4,5},{5,4},{6,7},{7,6},{8,9},{9,8},{10,11... | collective-permute-start | bytes 1769480 | tf_op jit(solution)/shard_map/ppermute | solution.py:790
  305.1 22.4 %collective-permute-start.24 = (bf16[4,48,768]{2,1,0:T(8,128)(2,1)S(1)}, bf16[4,48,768]{2,1,0:T(8,128)(2,1)S(1)}, u32[]{:S(2)}, u32[]{:S(2)}) collective-permute-start(bf16[4,48,768]{2,1,0:T(8,128)(2,1)S(1)} %get-tuple-element.187.refs_7_), channel_id=1, source_target_pairs={{0,2},{2,0},{1,3},{3,1},{4,6},{6,4},{5,7},{7,5},{8,10},{10,8},{9,1... | collective-permute-start | bytes 884744 | tf_op jit(solution)/shard_map/ppermute | solution.py:790
  306.9 20.7 %collective-permute-start.23 = (bf16[4,48,768]{2,1,0:T(8,128)(2,1)S(1)}, bf16[4,48,768]{2,1,0:T(8,128)(2,1)S(1)}, u32[]{:S(2)}, u32[]{:S(2)}) collective-permute-start(bf16[4,48,768]{2,1,0:T(8,128)(2,1)S(1)} %get-tuple-element.189.refs_6_), channel_id=1, source_target_pairs={{0,1},{1,0},{2,3},{3,2},{4,5},{5,4},{6,7},{7,6},{8,9},{9,8},{10,11... | collective-permute-start | bytes 884744 | tf_op jit(solution)/shard_map/ppermute | solution.py:790
  309.1 24.4 %collective-permute-start.29 = (bf16[48,3072]{1,0:T(8,128)(2,1)S(1)}, bf16[48,3072]{1,0:T(8,128)(2,1)S(1)}, u32[]{:S(2)}, u32[]{:S(2)}) collective-permute-start(bf16[48,3072]{1,0:T(8,128)(2,1)S(1)} %get-tuple-element.182), channel_id=1, source_target_pairs={{0,24},{4,28},{8,0},{12,4},{16,8},{20,12},{24,16},{28,20},{1,25},{... | collective-permute-start | bytes 884744 | tf_op jit(solution)/shard_map/ppermute | solution.py:801
  313.3 20.2 %collective-permute-start.27 = (bf16[48,3072]{1,0:T(8,128)(2,1)S(1)}, bf16[48,3072]{1,0:T(8,128)(2,1)S(1)}, u32[]{:S(2)}, u32[]{:S(2)}) collective-permute-start(bf16[48,3072]{1,0:T(8,128)(2,1)S(1)} %get-tuple-element.184), channel_id=1, source_target_pairs={{0,8},{4,12},{8,16},{12,20},{16,24},{20,28},{24,0},{28,4},{1,9},{5... | collective-permute-start | bytes 884744 | tf_op jit(solution)/shard_map/ppermute | solution.py:801
  313.3 33.9 %collective-permute-start.28 = (bf16[48,3072]{1,0:T(8,128)(2,1)S(1)}, bf16[48,3072]{1,0:T(8,128)(2,1)S(1)}, u32[]{:S(2)}, u32[]{:S(2)}) collective-permute-start(bf16[48,3072]{1,0:T(8,128)(2,1)S(1)} %get-tuple-element.185), channel_id=1, source_target_pairs={{0,16},{4,20},{8,24},{12,28},{16,0},{20,4},{24,8},{28,12},{1,17},{... | collective-permute-start | bytes 884744 | tf_op jit(solution)/shard_map/ppermute | solution.py:801
  328.4 18.8 %collective-permute-start.26 = (bf16[96,2432]{1,0:T(8,128)(2,1)}, bf16[96,2432]{1,0:T(8,128)(2,1)S(1)}, u32[]{:S(2)}, u32[]{:S(2)}) collective-permute-start(bf16[96,2432]{1,0:T(8,128)(2,1)} %get-tuple-element.145.refs_1_), channel_id=1, source_target_pairs={{0,2},{2,0},{1,3},{3,1},{4,6},{6,4},{5,7},{7,5},{8,10},{10,8},{9,1... | collective-permute-start | bytes 1400840 | tf_op jit(solution)/shard_map/ppermute | solution.py:790
  330.1 25.7 %collective-permute-start.25 = (bf16[512,768]{1,0:T(8,128)(2,1)}, bf16[512,768]{1,0:T(8,128)(2,1)S(1)}, u32[]{:S(2)}, u32[]{:S(2)}) collective-permute-start(bf16[512,768]{1,0:T(8,128)(2,1)} %get-tuple-element.142), channel_id=1, source_target_pairs={{0,2},{2,0},{1,3},{3,1},{4,6},{6,4},{5,7},{7,5},{8,10},{10,8},{9,1... | collective-permute-start | bytes 2359304 | tf_op jit(solution)/shard_map/ppermute | solution.py:787
  351.2 15.8 %collective-permute-start.31 = (bf16[48,1536]{1,0:T(8,128)(2,1)S(1)}, bf16[48,1536]{1,0:T(8,128)(2,1)S(1)}, u32[]{:S(2)}, u32[]{:S(2)}) collective-permute-start(bf16[48,1536]{1,0:T(8,128)(2,1)S(1)} %get-tuple-element.194), channel_id=1, source_target_pairs={{0,8},{4,12},{8,16},{12,20},{16,24},{20,28},{24,0},{28,4},{1,9},{5... | collective-permute-start | bytes 442376 | tf_op jit(solution)/shard_map/ppermute | solution.py:801
  (92 other events, 491.8 us)
Sparse Core Ops, SparseCore 0:
  10.3 117.3 all-gather.2
  272.3 50.0 reduce-scatter.2
  324.7 39.5 reduce-scatter.4
where the time goes:
time: 399 us; the launch traced here: 394 us
  Pallas kernels  178 us (45%)
  waiting for transfers between devices  68.6 us (17%)
  starting transfers between devices  51 us (13%)
  other arithmetic  48.5 us (12%)
  local copies, waits for them, and re-layouts  32.3 us (8%)
  between operations  16.2 us (4%)
    pallas_call x1, Pallas kernels, feed_forward(): pl.pallas_call(functools.partial(feed_kernel, plan), grid_spec=pltpu.Pref...  76.5 us
    pallas_call x3, Pallas kernels, attend_back(): pl.pallas_call(functools.partial(attend_back_kernel, len(waits)), grid_sp...  56.5 us
    ppermute x17, waiting for transfers between devices, swap(): return lax.ppermute(value, axis, [(0, 1), (1, 0)])  31.8 us
    ppermute x12, waiting for transfers between devices, shift(): return lax.ppermute(value, 'fsdp', pairs)  27.4 us
    ppermute x12, starting transfers between devices, shift(): return lax.ppermute(value, 'fsdp', pairs)  24.2 us
    pallas_call x1, Pallas kernels, attend(): pl.pallas_call(attend_kernel, grid_spec=pltpu.PrefetchScalarGridSpec(num_...  23.5 us
    ppermute x17, starting transfers between devices, swap(): return lax.ppermute(value, axis, [(0, 1), (1, 0)])  19.8 us
    convert_element_type x14, other arithmetic, add(): return (left.astype(f32) + right.astype(f32)).astype(bf16)  18.4 us
  transfers between devices with their start and end apart: 41, of which 15 were waited for; matrix products, arithmetic and copies ran while one was open for 15% of the time, Pallas kernels for 26%

commit v1 on v0

--- a/solution.py
+++ b/solution.py
@@ -1061,10 +1061,10 @@
 
         feed_core = move.swap_core(feed_send)
         other_mixed = move.swap_slots(mixed_send)
-        attn_a, raw_0 = back(0, 2, grad_context, (), attn_o)
+        attn_a, raw_0 = back(0, 1, grad_context, (), attn_o)
 
         raw_0, feed_keep, grad_context = fence(
-            raw_0, feed_keep, grad_context, waits=(feed_core, other_mixed)
+            raw_0, feed_keep, grad_context, waits=(feed_core,)
         )
         width = feed_width // 2
         shape = (3, 2, 2, levels, half, feed_width)
@@ -1086,10 +1086,10 @@
         down, gate = joined(0, (every, 0)), joined(1, (0,))
         up_a, up_b = joined(2, (every, 0) + first), joined(2, (0,) + last)
         sends = (down_send, gate_send, up_a_send, up_b_send)
-        attn_a, raw_1 = back(2, 2, grad_context, (raw_0, *sends), attn_a)
+        attn_a, raw_1 = back(1, 3, grad_context, (raw_0, *sends), attn_a)
 
         raw_1, attn_a, grad_context, down, gate = fence(
-            raw_1, attn_a, grad_context, down, gate, waits=(down_x, gate_y)
+            raw_1, attn_a, grad_context, down, gate, waits=(down_x, gate_y, other_mixed)
         )
         attn_a = move.sum_shards(attn_a)
         down_send, down = move.add(down[1], down_x[1]), move.add(down[0], down_x[0])
@@ -1122,9 +1122,14 @@
         )
         attn_x = move.swap(attn_a, "ctx")
         other_rows = move.swap_slots(send_rows)
-        up = jnp.concatenate([move.add(up_a, up_a_y), move.add(up_b, up_b_x)], 2)
-
-        up, attn_a, some = fence(up, attn_a, some, waits=(attn_x, *some_shifts))
+        up = [
+            jnp.concatenate(
+                [move.add(up_a[step], up_a_y[step]), move.add(up_b[step], up_b_x[step])], 1
+            )
+            for step in range(levels)
+        ]
+
+        attn_a, some, *up = fence(attn_a, some, *up, waits=(attn_x, *some_shifts))
         up_shifts = move.level_shifts(up)
         some = move.sum_shifts(some, some_shifts)
         attn_a = move.add(attn_a, attn_x)

time: 399 us -> 396 us (level)
  waiting for transfers between devices: 68.6 us -> 59.6 us
    unnamed x150 -> x148, local copies, waits for them, and re-layouts: 12.2 us -> 11.9 us
  transfers between devices with their start and end apart: 41 -> 41, of which waited for: 15 -> 13; matrix products, arithmetic and copies ran while one was open for 15% -> 17% of each run, Pallas kernels for 26% -> 26%
where the time goes in v1:
time: 396 us; the launch traced here: 389 us
  Pallas kernels  177 us (45%)
  waiting for transfers between devices  59.6 us (15%)
  starting transfers between devices  54.6 us (14%)
  other arithmetic  50.8 us (13%)
  local copies, waits for them, and re-layouts  30 us (8%)
  between operations  16.2 us (4%)
    pallas_call x1, Pallas kernels, feed_forward(): pl.pallas_call(functools.partial(feed_kernel, plan), grid_spec=pltpu.Pref...  76.5 us
    pallas_call x3, Pallas kernels, attend_back(): pl.pallas_call(functools.partial(attend_back_kernel, len(waits)), grid_sp...  56.3 us
    ppermute x17, waiting for transfers between devices, swap(): return lax.ppermute(value, axis, [(0, 1), (1, 0)])  28.3 us
    ppermute x12, starting transfers between devices, shift(): return lax.ppermute(value, 'fsdp', pairs)  26.4 us
    ppermute x12, waiting for transfers between devices, shift(): return lax.ppermute(value, 'fsdp', pairs)  23.9 us
    pallas_call x1, Pallas kernels, attend(): pl.pallas_call(attend_kernel, grid_spec=pltpu.PrefetchScalarGridSpec(num_...  23.5 us
    ppermute x17, starting transfers between devices, swap(): return lax.ppermute(value, axis, [(0, 1), (1, 0)])  19.9 us
    convert_element_type x14, other arithmetic, add(): return (left.astype(f32) + right.astype(f32)).astype(bf16)  18.9 us
  transfers between devices with their start and end apart: 41, of which 13 were waited for; matrix products, arithmetic and copies ran while one was open for 17% of the time, Pallas kernels for 26%

profile of v1, /device:TPU:0, one launch (start us, length us, event | category | flops | bytes accessed | tf_op | source)
XLA Modules:
  0.0 388.8 jit_solution(2046168138172485749)
XLA Ops:
  11.3 5.1 %collective-permute-start.2 = (bf16[48,1152]{1,0:T(8,128)(2,1)S(1)}, bf16[48,1152]{1,0:T(8,128)(2,1)S(1)}, u32[]{:S(2)}, u32[]{:S(2)}) collective-permute-start(bf16[48,1152]{1,0:T(8,128)(2,1)S(1)} %dynamic_slice.31.refs_1_), channel_id=1, source_target_pairs={{0,24},{4,28},{8,0},{12,4},{16,8},{20,12},{24,16},{28,20},{1,25},{... | collective-permute-start | bytes 331784 | tf_op jit(solution)/shard_map/ppermute | solution.py:801
  25.3 4.0 %collective-permute-done.1.refs_4_ = bf16[48,1152]{1,0:T(8,128)(2,1)S(1)} collective-permute-done((bf16[48,1152]{1,0:T(8,128)(2,1)S(1)}, bf16[48,1152]{1,0:T(8,128)(2,1)S(1)}, u32[]{:S(2)}, u32[]{:S(2)}) %collective-permute-start.1) | collective-permute-done | bytes 110624 | tf_op jit(solution)/shard_map/ppermute | solution.py:801
  35.4 2.9 collective-permute-done.4
  44.4 3.3 collective-permute-start.9
  47.7 3.6 collective-permute-start.8
  53.8 7.0 %collective-permute-done.8.refs_5_ = bf16[48,1536]{1,0:T(8,128)(2,1)S(1)} collective-permute-done((bf16[48,1536]{1,0:T(8,128)(2,1)S(1)}, bf16[48,1536]{1,0:T(8,128)(2,1)S(1)}, u32[]{:S(2)}, u32[]{:S(2)}) %collective-permute-start.8) | collective-permute-done | bytes 147488 | tf_op jit(solution)/shard_map/ppermute | solution.py:801
  71.0 10.1 %project.1 = (bf16[1024,768]{1,0:T(8,128)(2,1)}, bf16[1024,768]{1,0:T(8,128)(2,1)}, bf16[1024,768]{1,0:T(8,128)(2,1)}, bf16[768,1024]{1,0:T(8,128)(2,1)}) custom-call(s32[18]{0:T(128)} %stack.278.spots, bf16[1024,768]{1,0:T(8,128)(2,1)} %get-tuple-element.90.tokens, f32[1024,128]{1,0:T(8,128)} %get-tuple-element.91.cosine.cos_ref, ...), custom_call_target="tpu_custom_call" | custom-call | flops 3623878656 | bytes 12976128 | tf_op jit(solution)/shard_map/project/pallas_call | solution.py:129
  81.1 13.4 %collective-permute-done.11.refs_2_ = bf16[4,48,1536]{2,1,0:T(8,128)(2,1)S(1)} collective-permute-done((bf16[4,48,1536]{2,1,0:T(8,128)(2,1)S(1)}, bf16[4,48,1536]{2,1,0:T(8,128)(2,1)S(1)}, u32[]{:S(2)}, u32[]{:S(2)}) %collective-permute-start.11) | collective-permute-done | bytes 589856 | tf_op jit(solution)/shard_map/ppermute | solution.py:790
  97.7 23.5 %attend.1 = (bf16[1024,768]{1,0:T(8,128)(2,1)}, f32[6,1024,128]{2,1,0:T(8,128)}) custom-call(s32[1]{0:T(128)S(6)} %select_n.241.length, bf16[1024,768]{1,0:T(8,128)(2,1)} %get-tuple-element.104.q_ref, bf16[1024,768]{1,0:T(8,128)(2,1)} %get-tuple-element.105.k_ref, bf16[1024,768]{1,0:T(8,128)(2,1)} %get-tuple-element.106.v_ref), custom_call_target="tpu_custom_call" | custom-call | flops 12884901888 | bytes 9437184 | tf_op jit(solution)/shard_map/attend/pallas_call | solution.py:194
  121.2 3.1 collective-permute-done.12.refs_2_
  132.7 76.5 %feed_forward.1 = (bf16[512,768]{1,0:T(8,128)(2,1)}, bf16[512,768]{1,0:T(8,128)(2,1)}, f32[1024,768]{1,0:T(8,128)}, bf16[1024,768]{1,0:T(8,128)(2,1)}, bf16[768,...) custom-call(s32[1]{0:T(128)} %bitcast.slot_half, s32[18]{0:T(128)} %stack.257.spots_in, ...), custom_call_target="tpu_custom_call" | custom-call | flops 47110422528 | bytes 47185920 | tf_op jit(solution)/shard_map/feed_forward/pallas_call | solution.py:726
  210.5 10.8 %attend_back.3 = (bf16[768,2432]{1,0:T(8,128)(2,1)}, bf16[1024,384]{1,0:T(8,128)(2,1)}) custom-call(s32[1]{0:T(128)S(6)} %select_n.241.length, s32[1]{0:T(128)} %constant.222.clone.1.first, bf16[1024,768]{1,0:T(8,128)(2,1)} %get-tuple-element.104.q_ref, bf16[1024,768]{1,0:T(8,128)(2,1)} %get-tuple-element.105.k_ref, ...), custom_call_target="tpu_custom_call", output_to_operand_aliasing={{0}: (11, {})} | custom-call | flops 6174015488 | bytes 2097152 | tf_op jit(solution)/shard_map/attend_back/pallas_call | solution.py:329
  221.3 2.7 fusion.43
  224.0 2.7 fusion.44
  229.4 4.4 %add_convert_fusion = (bf16[1,1,8,48,1536]{4,3,2,1,0:T(8,128)(2,1)}, bf16[1,1,8,48,1536]{4,3,2,1,0:T(8,128)(2,1)}) fusion(bf16[3,2,8,48,1536]{4,3,2,1,0:T(8,128)(2,1)} %collective-permute-done.16.refs_3_, bf16[3,2,8,48,1536]{4,3,2,1,0:T(8,128)(2,1)} %get-tuple-element.127), kind=kLoop, calls=%fused_computation.2 | loop fusion | flops 4718592 | bytes 7077888 | tf_op jit(solution)/shard_map/convert_element_type | solution.py:865
  238.6 26.7 %attend_back.4 = (bf16[768,2432]{1,0:T(8,128)(2,1)}, bf16[1024,1152]{1,0:T(8,128)(2,1)}) custom-call(s32[1]{0:T(128)S(6)} %select_n.241.length, s32[1]{0:T(128)} %constant.223.clone.1.first, bf16[1024,768]{1,0:T(8,128)(2,1)} %get-tuple-element.104.q_ref, bf16[1024,768]{1,0:T(8,128)(2,1)} %get-tuple-element.105.k_ref, ...), custom_call_target="tpu_custom_call", output_to_operand_aliasing={{0}: (11, {})} | custom-call | flops 18522046464 | bytes 6291456 | tf_op jit(solution)/shard_map/attend_back/pallas_call | solution.py:329
  276.2 18.8 %attend_back.5 = (bf16[768,768]{1,0:T(8,128)(2,1)}, bf16[1024,768]{1,0:T(8,128)(2,1)}) custom-call(s32[1]{0:T(128)S(6)} %select_n.241.length, s32[1]{0:T(128)} %constant.224.clone.1.first, bf16[1024,768]{1,0:T(8,128)(2,1)} %get-tuple-element.104.q_ref, bf16[1024,768]{1,0:T(8,128)(2,1)} %get-tuple-element.105.k_ref, ...), custom_call_target="tpu_custom_call" | custom-call | flops 12348030976 | bytes 4194304 | tf_op jit(solution)/shard_map/attend_back/pallas_call | solution.py:329
  305.1 3.9 %collective-permute-start.29 = (bf16[48,3072]{1,0:T(8,128)(2,1)S(1)}, bf16[48,3072]{1,0:T(8,128)(2,1)S(1)}, u32[]{:S(2)}, u32[]{:S(2)}) collective-permute-start(bf16[48,3072]{1,0:T(8,128)(2,1)S(1)} %get-tuple-element.188), channel_id=1, source_target_pairs={{0,24},{4,28},{8,0},{12,4},{16,8},{20,12},{24,16},{28,20},{1,25},{... | collective-permute-start | bytes 884744 | tf_op jit(solution)/shard_map/ppermute | solution.py:801
  309.0 2.9 collective-permute-start.28
  313.0 11.1 %token_gradient.1 = (f32[512,768]{1,0:T(8,128)}, bf16[512,768]{1,0:T(8,128)(2,1)}) custom-call(s32[1]{0:T(128)} %bitcast.slot_half, s32[18]{0:T(128)} %stack.278.spots, bf16[1024,384]{1,0:T(8,128)(2,1)} %get-tuple-element.124.refs_1_.refs_0_, bf16[1024,1152]{1,0:T(8,128)(2,1)} %get-tuple-element.130.refs_1_, bf16[1024,768]{1,0:T(8,128)(2,1)} %get-tuple-element.136.refs_2_, ...), custom_call_target="tpu_custom_call" | custom-call | flops 3623878656 | bytes 14548992 | tf_op jit(solution)/shard_map/token_gradient/pallas_call | solution.py:418
  332.1 10.9 %collective-permute-done.28.refs_8_ = bf16[48,3072]{1,0:T(8,128)(2,1)S(1)} collective-permute-done((bf16[48,3072]{1,0:T(8,128)(2,1)S(1)}, bf16[48,3072]{1,0:T(8,128)(2,1)S(1)}, u32[]{:S(2)}, u32[]{:S(2)}) %collective-permute-start.28) | collective-permute-done | bytes 294944 | tf_op jit(solution)/shard_map/ppermute | solution.py:801
  345.3 2.6 collective-permute-start.33
  354.3 4.5 %reduce-scatter.5.cloned.1.call-done.refs_2_ = bf16[96,768]{1,0:T(8,128)(2,1)} async-done(((bf16[768,768]{1,0:T(8,128)(2,1)}), bf16[96,768]{1,0:T(8,128)(2,1)}) %reduce-scatter.5.cloned.1.call-update) | async-done | bytes 147472 | tf_op jit(solution)/shard_map/reduce_scatter | solution.py:877
  374.2 6.2 %collective-permute-done.37 = bf16[48,4608]{1,0:T(8,128)(2,1)S(1)} collective-permute-done((bf16[48,4608]{1,0:T(8,128)(2,1)S(1)}, bf16[48,4608]{1,0:T(8,128)(2,1)S(1)}, u32[]{:S(2)}, u32[]{:S(2)}) %collective-permute-start.37) | collective-permute-done | bytes 442400 | tf_op jit(solution)/shard_map/ppermute | solution.py:790
  (298 shorter events, 111.7 us)
Async XLA Ops:
  7.2 124.1 %all-gather.3.cloned.1.call-start = ((), (), s32[]{:S(2)}) async-start(), calls=%async_computation.4 | async-start | bytes 11698176 | tf_op jit(solution)/shard_map/all_gather | solution.py:834
  10.2 314.0 %reduce-scatter.3.cloned.1.call-start = ((), (), s32[]{:S(2)}) async-start(), calls=%async_computation.2 | async-start | bytes 4202496 | tf_op jit(solution)/shard_map/reduce_scatter | solution.py:877
  19.9 18.4 %collective-permute-start.4 = (bf16[512,768]{1,0:T(8,128)(2,1)}, bf16[512,768]{1,0:T(8,128)(2,1)S(1)}, u32[]{:S(2)}, u32[]{:S(2)}) collective-permute-start(bf16[512,768]{1,0:T(8,128)(2,1)} %dynamic-slice_bitcast_fusion), channel_id=1, source_target_pairs={{0,2},{2,0},{1,3},{3,1},{4,6},{6,4},{5,7},{7,5},{8,10},{10,8},{9,1... | collective-permute-start | bytes 2359304 | tf_op jit(solution)/shard_map/ppermute | solution.py:787
  42.8 18.4 %collective-permute-start.6 = (bf16[2,4,48,1152]{3,2,1,0:T(8,128)(2,1)S(1)}, bf16[2,4,48,1152]{3,2,1,0:T(8,128)(2,1)S(1)}, u32[]{:S(2)}, u32[]{:S(2)}) collective-permute-start(bf16[2,4,48,1152]{3,2,1,0:T(8,128)(2,1)S(1)} %pad_maximum_fusion.6.refs_0_), channel_id=1, source_target_pairs={{0,2},{2,0},{1,3},{3,1},{4,6},{6,4},{5,7},{7,5},{8,10},{10,8},{9,1... | collective-permute-start | bytes 2654216 | tf_op jit(solution)/shard_map/ppermute | solution.py:790
  65.7 28.7 %collective-permute-start.11 = (bf16[4,48,1536]{2,1,0:T(8,128)(2,1)S(1)}, bf16[4,48,1536]{2,1,0:T(8,128)(2,1)S(1)}, u32[]{:S(2)}, u32[]{:S(2)}) collective-permute-start(bf16[4,48,1536]{2,1,0:T(8,128)(2,1)S(1)} %pad_maximum_fusion.7.refs_1_), channel_id=1, source_target_pairs={{0,1},{1,0},{2,3},{3,2},{4,5},{5,4},{6,7},{7,6},{8,9},{9,8},{10,11... | collective-permute-start | bytes 1769480 | tf_op jit(solution)/shard_map/ppermute | solution.py:790
  69.7 51.5 %collective-permute-start.13 = (bf16[512,768]{1,0:T(8,128)(2,1)S(1)}, bf16[512,768]{1,0:T(8,128)(2,1)S(1)}, u32[]{:S(2)}, u32[]{:S(2)}) collective-permute-start(bf16[512,768]{1,0:T(8,128)(2,1)S(1)} %copy-done.6), channel_id=1, source_target_pairs={{0,2},{2,0},{1,3},{3,1},{4,6},{6,4},{5,7},{7,5},{8,10},{10,8},{9,1... | collective-permute-start | bytes 2359304 | tf_op jit(solution)/shard_map/ppermute | solution.py:787
  96.6 27.7 %collective-permute-start.12 = (bf16[2,4,48,1536]{3,2,1,0:T(8,128)(2,1)S(1)}, bf16[2,4,48,1536]{3,2,1,0:T(8,128)(2,1)S(1)}, u32[]{:S(2)}, u32[]{:S(2)}) collective-permute-start(bf16[2,4,48,1536]{3,2,1,0:T(8,128)(2,1)S(1)} %pad_maximum_fusion.5.refs_1_), channel_id=1, source_target_pairs={{0,2},{2,0},{1,3},{3,1},{4,6},{6,4},{5,7},{7,5},{8,10},{10,8},{9,1... | collective-permute-start | bytes 3538952 | tf_op jit(solution)/shard_map/ppermute | solution.py:790
  209.7 55.6 %collective-permute-start.15 = (bf16[512,768]{1,0:T(8,128)(2,1)}, bf16[512,768]{1,0:T(8,128)(2,1)S(1)}, u32[]{:S(2)}, u32[]{:S(2)}) collective-permute-start(bf16[512,768]{1,0:T(8,128)(2,1)} %get-tuple-element.116), channel_id=1, source_target_pairs={{0,2},{2,0},{1,3},{3,1},{4,6},{6,4},{5,7},{7,5},{8,10},{10,8},{9,1... | collective-permute-start | bytes 2359304 | tf_op jit(solution)/shard_map/ppermute | solution.py:787
  233.9 31.4 %collective-permute-start.18 = (bf16[2,4,48,1536]{3,2,1,0:T(8,128)(2,1)}, bf16[2,4,48,1536]{3,2,1,0:T(8,128)(2,1)S(1)}, u32[]{:S(2)}, u32[]{:S(2)}) collective-permute-start(bf16[2,4,48,1536]{3,2,1,0:T(8,128)(2,1)} %bitcast.70.refs_3_), channel_id=1, source_target_pairs={{0,1},{1,0},{2,3},{3,2},{4,5},{5,4},{6,7},{7,6},{8,9},{9,8},{10,11... | collective-permute-start | bytes 3538952 | tf_op jit(solution)/shard_map/ppermute | solution.py:790
  237.7 27.7 %collective-permute-start.17 = (bf16[2,4,48,1536]{3,2,1,0:T(8,128)(2,1)}, bf16[2,4,48,1536]{3,2,1,0:T(8,128)(2,1)S(1)}, u32[]{:S(2)}, u32[]{:S(2)}) collective-permute-start(bf16[2,4,48,1536]{3,2,1,0:T(8,128)(2,1)} %get-tuple-element.176.refs_2_), channel_id=1, source_target_pairs={{0,2},{2,0},{1,3},{3,1},{4,6},{6,4},{5,7},{7,5},{8,10},{10,8},{9,1... | collective-permute-start | bytes 3538952 | tf_op jit(solution)/shard_map/ppermute | solution.py:790
  267.0 91.8 %reduce-scatter.5.cloned.1.call-start = ((), (), s32[]{:S(2)}) async-start(), calls=%async_computation.3 | async-start | bytes 1327104 | tf_op jit(solution)/shard_map/reduce_scatter | solution.py:877
  269.7 25.3 %collective-permute-start.22 = (bf16[2,4,48,768]{3,2,1,0:T(8,128)(2,1)S(1)}, bf16[2,4,48,768]{3,2,1,0:T(8,128)(2,1)S(1)}, u32[]{:S(2)}, u32[]{:S(2)}) collective-permute-start(bf16[2,4,48,768]{3,2,1,0:T(8,128)(2,1)S(1)} %copy-done.61), channel_id=1, source_target_pairs={{0,1},{1,0},{2,3},{3,2},{4,5},{5,4},{6,7},{7,6},{8,9},{9,8},{10,11... | collective-permute-start | bytes 1769480 | tf_op jit(solution)/shard_map/ppermute | solution.py:790
  270.5 24.5 %collective-permute-start.21 = (bf16[2,4,48,768]{3,2,1,0:T(8,128)(2,1)S(1)}, bf16[2,4,48,768]{3,2,1,0:T(8,128)(2,1)S(1)}, u32[]{:S(2)}, u32[]{:S(2)}) collective-permute-start(bf16[2,4,48,768]{3,2,1,0:T(8,128)(2,1)S(1)} %copy-done.60), channel_id=1, source_target_pairs={{0,2},{2,0},{1,3},{3,1},{4,6},{6,4},{5,7},{7,5},{8,10},{10,8},{9,1... | collective-permute-start | bytes 1769480 | tf_op jit(solution)/shard_map/ppermute | solution.py:790
  272.4 25.0 %collective-permute-start.20 = (bf16[4,48,1536]{2,1,0:T(8,128)(2,1)S(1)}, bf16[4,48,1536]{2,1,0:T(8,128)(2,1)S(1)}, u32[]{:S(2)}, u32[]{:S(2)}) collective-permute-start(bf16[4,48,1536]{2,1,0:T(8,128)(2,1)S(1)} %get-tuple-element.178.refs_1_), channel_id=1, source_target_pairs={{0,2},{2,0},{1,3},{3,1},{4,6},{6,4},{5,7},{7,5},{8,10},{10,8},{9,1... | collective-permute-start | bytes 1769480 | tf_op jit(solution)/shard_map/ppermute | solution.py:790
  275.0 22.4 %collective-permute-start.19 = (bf16[4,48,1536]{2,1,0:T(8,128)(2,1)}, bf16[4,48,1536]{2,1,0:T(8,128)(2,1)S(1)}, u32[]{:S(2)}, u32[]{:S(2)}) collective-permute-start(bf16[4,48,1536]{2,1,0:T(8,128)(2,1)} %get-tuple-element.180.refs_0_), channel_id=1, source_target_pairs={{0,1},{1,0},{2,3},{3,2},{4,5},{5,4},{6,7},{7,6},{8,9},{9,8},{10,11... | collective-permute-start | bytes 1769480 | tf_op jit(solution)/shard_map/ppermute | solution.py:790
  300.6 23.5 %collective-permute-start.24 = (bf16[4,48,768]{2,1,0:T(8,128)(2,1)S(1)}, bf16[4,48,768]{2,1,0:T(8,128)(2,1)S(1)}, u32[]{:S(2)}, u32[]{:S(2)}) collective-permute-start(bf16[4,48,768]{2,1,0:T(8,128)(2,1)S(1)} %get-tuple-element.193.refs_7_), channel_id=1, source_target_pairs={{0,2},{2,0},{1,3},{3,1},{4,6},{6,4},{5,7},{7,5},{8,10},{10,8},{9,1... | collective-permute-start | bytes 884744 | tf_op jit(solution)/shard_map/ppermute | solution.py:790
  302.5 21.7 %collective-permute-start.23 = (bf16[4,48,768]{2,1,0:T(8,128)(2,1)S(1)}, bf16[4,48,768]{2,1,0:T(8,128)(2,1)S(1)}, u32[]{:S(2)}, u32[]{:S(2)}) collective-permute-start(bf16[4,48,768]{2,1,0:T(8,128)(2,1)S(1)} %get-tuple-element.195.refs_6_), channel_id=1, source_target_pairs={{0,1},{1,0},{2,3},{3,2},{4,5},{5,4},{6,7},{7,6},{8,9},{9,8},{10,11... | collective-permute-start | bytes 884744 | tf_op jit(solution)/shard_map/ppermute | solution.py:790
  305.1 27.0 %collective-permute-start.29 = (bf16[48,3072]{1,0:T(8,128)(2,1)S(1)}, bf16[48,3072]{1,0:T(8,128)(2,1)S(1)}, u32[]{:S(2)}, u32[]{:S(2)}) collective-permute-start(bf16[48,3072]{1,0:T(8,128)(2,1)S(1)} %get-tuple-element.188), channel_id=1, source_target_pairs={{0,24},{4,28},{8,0},{12,4},{16,8},{20,12},{24,16},{28,20},{1,25},{... | collective-permute-start | bytes 884744 | tf_op jit(solution)/shard_map/ppermute | solution.py:801
  309.0 23.1 %collective-permute-start.27 = (bf16[48,3072]{1,0:T(8,128)(2,1)S(1)}, bf16[48,3072]{1,0:T(8,128)(2,1)S(1)}, u32[]{:S(2)}, u32[]{:S(2)}) collective-permute-start(bf16[48,3072]{1,0:T(8,128)(2,1)S(1)} %get-tuple-element.190), channel_id=1, source_target_pairs={{0,8},{4,12},{8,16},{12,20},{16,24},{20,28},{24,0},{28,4},{1,9},{5... | collective-permute-start | bytes 884744 | tf_op jit(solution)/shard_map/ppermute | solution.py:801
  309.0 34.0 %collective-permute-start.28 = (bf16[48,3072]{1,0:T(8,128)(2,1)S(1)}, bf16[48,3072]{1,0:T(8,128)(2,1)S(1)}, u32[]{:S(2)}, u32[]{:S(2)}) collective-permute-start(bf16[48,3072]{1,0:T(8,128)(2,1)S(1)} %get-tuple-element.191), channel_id=1, source_target_pairs={{0,16},{4,20},{8,24},{12,28},{16,0},{20,4},{24,8},{28,12},{1,17},{... | collective-permute-start | bytes 884744 | tf_op jit(solution)/shard_map/ppermute | solution.py:801
  324.9 18.1 %collective-permute-start.26 = (bf16[96,2432]{1,0:T(8,128)(2,1)}, bf16[96,2432]{1,0:T(8,128)(2,1)S(1)}, u32[]{:S(2)}, u32[]{:S(2)}) collective-permute-start(bf16[96,2432]{1,0:T(8,128)(2,1)} %get-tuple-element.146.refs_0_), channel_id=1, source_target_pairs={{0,2},{2,0},{1,3},{3,1},{4,6},{6,4},{5,7},{7,5},{8,10},{10,8},{9,1... | collective-permute-start | bytes 1400840 | tf_op jit(solution)/shard_map/ppermute | solution.py:790
  326.0 25.8 %collective-permute-start.25 = (bf16[512,768]{1,0:T(8,128)(2,1)}, bf16[512,768]{1,0:T(8,128)(2,1)S(1)}, u32[]{:S(2)}, u32[]{:S(2)}) collective-permute-start(bf16[512,768]{1,0:T(8,128)(2,1)} %get-tuple-element.145), channel_id=1, source_target_pairs={{0,2},{2,0},{1,3},{3,1},{4,6},{6,4},{5,7},{7,5},{8,10},{10,8},{9,1... | collective-permute-start | bytes 2359304 | tf_op jit(solution)/shard_map/ppermute | solution.py:787
  344.0 16.6 %collective-permute-start.32 = (bf16[48,1536]{1,0:T(8,128)(2,1)}, bf16[48,1536]{1,0:T(8,128)(2,1)S(1)}, u32[]{:S(2)}, u32[]{:S(2)}) collective-permute-start(bf16[48,1536]{1,0:T(8,128)(2,1)} %get-tuple-element.155), channel_id=1, source_target_pairs={{0,16},{4,20},{8,24},{12,28},{16,0},{20,4},{24,8},{28,12},{1,17},{... | collective-permute-start | bytes 442376 | tf_op jit(solution)/shard_map/ppermute | solution.py:801
  345.3 15.3 %collective-permute-start.33 = (bf16[48,1536]{1,0:T(8,128)(2,1)}, bf16[48,1536]{1,0:T(8,128)(2,1)S(1)}, u32[]{:S(2)}, u32[]{:S(2)}) collective-permute-start(bf16[48,1536]{1,0:T(8,128)(2,1)} %get-tuple-element.156), channel_id=1, source_target_pairs={{0,24},{4,28},{8,0},{12,4},{16,8},{20,12},{24,16},{28,20},{1,25},{... | collective-permute-start | bytes 442376 | tf_op jit(solution)/shard_map/ppermute | solution.py:801
  (91 other events, 482.6 us)
Sparse Core Ops, SparseCore 0:
  10.3 117.3 all-gather.2
  267.1 49.2 reduce-scatter.2
  318.7 39.9 reduce-scatter.4
